TPU v7x, 128 devices: a whole 4x4x4 slice. The times are simulated.
128 devices in a mesh: tile: 128 (over z, x, y, core).
Axes of the slice: x: 4, y: 4, z: 4, core: 2. Of those that a mesh axis runs over, the one named last changes fastest.
Arguments:
- air_state: float32 [8, 1024, 128], P(None, 'tile'), may hold values from -6 to 6
- sea_state: float32 [48, 256, 512], P(None, 'tile'), may hold values from -6 to 6
- flux_start: float32 [4, 1024, 128], P(None, 'tile'), may hold values from -6 to 6
- air_cells: int32 [128, 5, 1024], P('tile'), may hold values from 0 to 1023
- sea_cells: int32 [128, 5, 1024], P('tile'), may hold values from 0 to 1023
- slot_counts: int32 [128, 5], P('tile'), may hold values from 0 to 1024, as said below
- sea_share: float32 [128, 5, 1024], P('tile'), may hold values from 0.2 to 1
- air_share: float32 [128, 5, 1024], P('tile'), may hold values from 0.2 to 1
- polar_fold_partner: int32 [512], replicated, may hold values from 0 to 511, each once
- wet_mask: int32 [256, 512], P('tile'), may hold values 0 or 1
- air_cotangent: float32 [8, 1024, 128], P(None, 'tile'), may hold values from -6 to 6
- sea_cotangent: float32 [48, 256, 512], P(None, 'tile'), may hold values from -6 to 6
- air_encoder: bfloat16 [64, 81], replicated, may hold values from -0.625 to 0.625
- air_depthwise: bfloat16 [64, 9], replicated, may hold values from -2 to 2
- air_expand: bfloat16 [256, 64], replicated, may hold values from -0.75 to 0.75
- air_contract: bfloat16 [64, 256], replicated, may hold values from -0.375 to 0.375
- air_decoder: bfloat16 [12, 64], replicated, may hold values from -0.75 to 0.75
- sea_encoder: bfloat16 [64, 468], replicated, may hold values from -0.25 to 0.25
- sea_depthwise: bfloat16 [64, 9], replicated, may hold values from -2 to 2
- sea_expand: bfloat16 [256, 64], replicated, may hold values from -0.75 to 0.75
- sea_contract: bfloat16 [64, 256], replicated, may hold values from -0.375 to 0.375
- sea_decoder: bfloat16 [48, 64], replicated, may hold values from -0.75 to 0.75
Outputs:
- air_final: float32 [8, 1024, 128], P(None, 'tile')
- sea_final: float32 [48, 256, 512], P(None, 'tile')
- air_grad: float32 [8, 1024, 128], P(None, 'tile')
- sea_grad: float32 [48, 256, 512], P(None, 'tile')
- flux_grad: float32 [4, 1024, 128], P(None, 'tile')
- air_encoder_grad: float32 [64, 81], replicated
- air_depthwise_grad: float32 [64, 9], replicated
- air_expand_grad: float32 [256, 64], replicated
- air_contract_grad: float32 [64, 256], replicated
- air_decoder_grad: float32 [12, 64], replicated
- sea_encoder_grad: float32 [64, 468], replicated
- sea_depthwise_grad: float32 [64, 9], replicated
- sea_expand_grad: float32 [256, 64], replicated
- sea_contract_grad: float32 [64, 256], replicated
- sea_decoder_grad: float32 [48, 64], replicated
Inputs may be any that keep to these rules, and one draw needn't show every extreme that they name: `slot_counts`: the number of used slots of each block, from its first slot on; 0 exactly for blocks whose atmosphere band lies off the grid, at least 256 for all others; in every draw some ocean band has 1024 used slots in every block with an atmosphere band on the grid, and some atmosphere band has 1024 used slots with every ocean band that it is paired with. `air_cells`: a cell of atmosphere band a, numbered row * 128 + column within the band. `sea_cells`: a cell of ocean band o, numbered row * 512 + column within the band. `polar_fold_partner`: each column appears once. `wet_mask`: 1 at ocean cells, 0 on land.
All inputs are finite; a program needn't handle non-finite values. No bound on the sum of `wet_mask` on one device may be relied on, other than what follows from the above.
Results may differ from a plain program's by a relative error of at most 0.025.
Values may be sent and summed in bfloat16 or wider, within the bound.
A program may use at most 128 MiB of HBM per device.

v0:
```python
from functools import partial
import math

import jax
import jax.numpy as jnp
from jax import lax
from jax.sharding import PartitionSpec as P

STEPS = 2


def passed_along(shard, axis, by):
    length = lax.axis_size(axis)
    pairs = [(i, i + by) for i in range(length) if 0 <= i + by < length]
    return lax.ppermute(shard, axis, pairs)


def with_halo(cells, sides, width):
    for axis, dim in sides:
        count = lax.axis_size(axis)
        ends = count - 1
        head = lax.slice_in_dim(cells, 0, width, axis=dim)
        tail = lax.slice_in_dim(cells, cells.shape[dim] - width, cells.shape[dim], axis=dim)
        cells = jnp.concatenate(
            [
                lax.ppermute(tail, axis, [(i, (i + 1) % count) for i in range(ends)]),
                cells,
                lax.ppermute(head, axis, [((i + 1) % count, i) for i in range(ends)]),
            ],
            axis=dim,
        )
    return cells


def taps(extended):
    rows = extended.shape[1] - 2
    pieces = []
    for shift_row in range(3):
        part = extended[:, shift_row : shift_row + rows]
        for shift_col in (-1, 0, 1):
            pieces.append(jnp.roll(part, -shift_col, axis=2))
    return pieces


def encode(encoder, extended):
    stacked = jnp.concatenate(taps(extended), axis=0)
    inputs, rows, width = stacked.shape
    product = jnp.dot(
        encoder.astype(jnp.bfloat16),
        stacked.reshape(inputs, rows * width),
        preferred_element_type=jnp.float32,
    )
    return product.astype(jnp.bfloat16).reshape(-1, rows, width)


def block(params, padded):
    depthwise, expand, contract, decoder = params
    pieces = taps(padded)
    mixed = pieces[0] * depthwise[:, 0][:, None, None]
    for tap in range(1, 9):
        mixed = mixed + pieces[tap] * depthwise[:, tap][:, None, None]
    channels, rows, width = mixed.shape
    flat = mixed.reshape(channels, rows * width)
    centred = flat - jnp.mean(flat, axis=0, keepdims=True)
    normed = centred * lax.rsqrt(jnp.mean(centred * centred, axis=0, keepdims=True) + 1e-06)
    hidden = jax.nn.gelu(
        jnp.dot(
            expand.astype(jnp.bfloat16),
            normed.astype(jnp.bfloat16),
            preferred_element_type=jnp.float32,
        ),
        approximate=True,
    ).astype(jnp.bfloat16)
    residual = padded[:, 1:-1].reshape(channels, rows * width) + jnp.dot(
        contract.astype(jnp.bfloat16), hidden, preferred_element_type=jnp.float32
    )
    output = jnp.dot(
        decoder.astype(jnp.bfloat16),
        residual.astype(jnp.bfloat16),
        preferred_element_type=jnp.float32,
    )
    return output.reshape(-1, rows, width)


def fold_top(extended, last, partner, width):
    mirrored = jnp.stack([extended[:, -width - 1][:, partner]], axis=1)
    return extended.at[:, -width:].set(jnp.where(last, mirrored, extended[:, -width:]))


def encode_layered(encoder, extended, last, folded, partner):
    if folded:
        extended = fold_top(extended, last, partner, 1)
    return encode(encoder, extended)


def block_layered(params, padded, last, folded, partner):
    if folded:
        padded = fold_top(padded, last, partner, 1)
    return block(params, padded)


def edge_rows(cotangent, width):
    return jnp.concatenate([cotangent[:, :width], cotangent[:, -width:]], axis=1)


def add_rims(inner, returned, width):
    inner = inner.at[:, :width].add(returned[:, :width].astype(jnp.float32))
    return inner.at[:, -width:].add(returned[:, -width:].astype(jnp.float32))


def body(
    air_state,
    sea_state,
    flux_start,
    air_cells,
    sea_cells,
    slot_counts,
    sea_share,
    air_share,
    polar_fold_partner,
    wet_mask,
    air_cotangent,
    sea_cotangent,
    air_encoder,
    air_depthwise,
    air_expand,
    air_contract,
    air_decoder,
    sea_encoder,
    sea_depthwise,
    sea_expand,
    sea_contract,
    sea_decoder,
):
    devices = lax.axis_size("tile")
    position = lax.axis_index("tile")
    last = position == devices - 1
    air_channels = air_state.shape[0]
    sea_channels = sea_state.shape[0]
    flux_channels = flux_start.shape[0]
    air_latitude_total, air_longitude_total = (air_state.shape[1], air_state.shape[2])
    sea_rows, sea_cols = (sea_state.shape[1], sea_state.shape[2])
    atmosphere_exchange_slots = air_cells[0]
    sea_slots = sea_cells[0]
    near_blocks = sea_slots.shape[0]
    centre = (near_blocks - 1) // 2
    slot_count = sea_slots.shape[1]
    used = (jnp.arange(slot_count, dtype=jnp.int32)[None, :] < slot_counts[0][:, None]).astype(
        jnp.float32
    )
    interpolate_to_sky = air_share[0] * used
    toward_sea = sea_share[0] * used
    wet = wet_mask.astype(jnp.float32)

    def route(ocean_blocks, air_blocks, backward):
        at_air = [None] * near_blocks
        at_sea = [None] * near_blocks
        for index in range(near_blocks):
            offset = index - centre
            mirror = near_blocks - 1 - index
            if offset == 0:
                at_air[index] = ocean_blocks[:, index]
                at_sea[index] = air_blocks[:, index]
            else:
                if backward:
                    moved = passed_along(
                        (ocean_blocks[:, index], air_blocks[:, mirror]), "tile", offset
                    )
                else:
                    moved = passed_along(
                        (ocean_blocks[:, index], air_blocks[:, mirror]), "tile", offset
                    )
                at_air[index] = moved[0]
                at_sea[mirror] = moved[1]
        return (jnp.stack(at_air, axis=1), jnp.stack(at_sea, axis=1))

    def forward_model(inputs, weights, folded):
        lowered = inputs.astype(jnp.bfloat16)
        if folded:
            extended = with_halo(lowered, (("tile", 1),), 1)
        else:
            extended = with_halo(lowered, (("tile", 1),), 1)
        encoder_local = partial(
            encode_layered, last=last, folded=folded, partner=polar_fold_partner
        )
        block_local = partial(block_layered, last=last, folded=folded, partner=polar_fold_partner)
        features, encoder_back = jax.vjp(encoder_local, weights[0], extended)
        if folded:
            padded = with_halo(features, (("tile", 1),), 1)
        else:
            padded = with_halo(features, (("tile", 1),), 1)
        outputs, block_back = jax.vjp(block_local, weights[1:], padded.astype(jnp.float32))

        def backward(cotangent):
            block_grads, padded_cotangent = block_back(cotangent)
            if folded:
                returned = with_halo(
                    edge_rows(padded_cotangent, 1).astype(jnp.bfloat16), (("tile", 1),), 1
                ).astype(jnp.float32)
            else:
                returned = with_halo(
                    edge_rows(padded_cotangent, 1).astype(jnp.bfloat16), (("tile", 1),), 1
                ).astype(jnp.float32)
            feature_cotangent = add_rims(padded_cotangent[:, 1:-1], returned, 1)
            encoder_grad, input_cotangent = encoder_back(feature_cotangent.astype(jnp.bfloat16))
            if folded:
                back_in = with_halo(edge_rows(input_cotangent, 1), (("tile", 1),), 1)
            else:
                back_in = with_halo(edge_rows(input_cotangent, 1), (("tile", 1),), 1)
            return (
                (encoder_grad,) + tuple(block_grads),
                add_rims(input_cotangent[:, 1:-1].astype(jnp.float32), back_in, 1),
            )

        return (outputs, backward)

    atmosphere_weight_set = tuple(
        (
            weight.astype(jnp.float32)
            for weight in (air_encoder, air_depthwise, air_expand, air_contract, air_decoder)
        )
    )
    sea_weights = tuple(
        (
            weight.astype(jnp.float32)
            for weight in (sea_encoder, sea_depthwise, sea_expand, sea_contract, sea_decoder)
        )
    )
    air_present_state, sea_now, flux_now = (air_state, sea_state, flux_start)
    record = []
    for step in range(STEPS):
        surface_flat = sea_now[0].reshape(-1)
        flux_flat = flux_now.reshape(flux_channels, -1)
        couple_at_air, couple_at_sea = route(
            (interpolate_to_sky * surface_flat[sea_slots])[None],
            flux_flat[:, atmosphere_exchange_slots],
            False,
        )
        skin_heat_level = (
            jnp.zeros((air_latitude_total * air_longitude_total,), jnp.float32)
            .at[atmosphere_exchange_slots.reshape(-1)]
            .add(couple_at_air[0].reshape(-1))
        )
        inbound_energy_map = (
            jnp.zeros((flux_channels, sea_rows * sea_cols), jnp.float32)
            .at[:, sea_slots.reshape(-1)]
            .add((toward_sea[None] * couple_at_sea).reshape(flux_channels, -1))
        )
        skin_heat_level, inbound_energy_map = (
            skin_heat_level.reshape(air_latitude_total, air_longitude_total),
            inbound_energy_map.reshape(flux_channels, sea_rows, sea_cols),
        )
        air_result_state, air_back = forward_model(
            jnp.concatenate([air_present_state, skin_heat_level[None]], axis=0),
            atmosphere_weight_set,
            False,
        )
        sea_out, sea_back = forward_model(
            jnp.concatenate([sea_now, inbound_energy_map], axis=0), sea_weights, True
        )
        record.append((air_back, sea_back))
        flux_now = air_result_state[air_channels:]
        air_present_state = air_present_state + air_result_state[:air_channels]
        sea_now = sea_now + wet[None] * sea_out
    air_total = tuple((jnp.zeros_like(weight) for weight in atmosphere_weight_set))
    sea_total = tuple((jnp.zeros_like(weight) for weight in sea_weights))
    air_cot = air_cotangent
    sea_cot = sea_cotangent
    flux_cot = jnp.zeros_like(flux_now)
    for step in range(STEPS - 1, -1, -1):
        air_back, sea_back = record[step]
        air_grads, air_inputs = air_back(jnp.concatenate([air_cot, flux_cot], axis=0))
        sea_grads, sea_inputs = sea_back(wet[None] * sea_cot)
        air_total = tuple((total + grad for total, grad in zip(air_total, air_grads)))
        sea_total = tuple((total + grad for total, grad in zip(sea_total, sea_grads)))
        inflow_flat = sea_inputs[sea_channels:].reshape(flux_channels, -1)
        coupler_at_air, coupler_at_sea = route(
            toward_sea[None] * inflow_flat[:, sea_slots],
            air_inputs[air_channels].reshape(-1)[atmosphere_exchange_slots][None],
            True,
        )
        interface_transfer_map = (
            jnp.zeros((sea_rows * sea_cols,), jnp.float32)
            .at[sea_slots.reshape(-1)]
            .add((interpolate_to_sky * coupler_at_sea[0]).reshape(-1))
        )
        fluxes = (
            jnp.zeros((flux_channels, air_latitude_total * air_longitude_total), jnp.float32)
            .at[:, atmosphere_exchange_slots.reshape(-1)]
            .add(coupler_at_air.reshape(flux_channels, -1))
        )
        surface_part = interface_transfer_map.reshape(sea_rows, sea_cols)
        flux_cot = fluxes.reshape(flux_channels, air_latitude_total, air_longitude_total)
        air_cot = air_cot + air_inputs[:air_channels]
        sea_cot = (sea_cot + sea_inputs[:sea_channels]).at[0].add(surface_part)
    summed = lax.psum(air_total + sea_total, "tile")
    air_scale = 1.0 / math.sqrt(air_latitude_total * air_longitude_total * devices)
    sea_scale = 1.0 / math.sqrt(sea_rows * sea_cols * devices)
    return (
        air_present_state,
        sea_now,
        air_cot,
        sea_cot,
        flux_cot,
        summed[0] * air_scale,
        summed[1] * air_scale,
        summed[2] * air_scale,
        summed[3] * air_scale,
        summed[4] * air_scale,
        summed[5] * sea_scale,
        summed[6] * sea_scale,
        summed[7] * sea_scale,
        summed[8] * sea_scale,
        summed[9] * sea_scale,
    )


def solution(mesh):
    placed = (
        P(None, "tile", None),
        P(None, "tile", None),
        P(None, "tile", None),
        P("tile", None, None),
        P("tile", None, None),
        P("tile", None),
        P("tile", None, None),
        P("tile", None, None),
        P(),
        P("tile", None),
        P(None, "tile", None),
        P(None, "tile", None),
        P(),
        P(),
        P(),
        P(),
        P(),
        P(),
        P(),
        P(),
        P(),
        P(),
    )
    return jax.shard_map(
        body,
        mesh=mesh,
        in_specs=placed,
        out_specs=(
            P(None, "tile", None),
            P(None, "tile", None),
            P(None, "tile", None),
            P(None, "tile", None),
            P(None, "tile", None),
            P(),
            P(),
            P(),
            P(),
            P(),
            P(),
            P(),
            P(),
            P(),
            P(),
        ),
        check_vma=False,
    )
```

profile of v0, /device:TPU:33, one launch (start us, length us, event | category | flops | bytes accessed | tf_op | source)
XLA Modules:
  0.0 1030.0 jit_solution(14549357642265090168)
XLA Ops:
  10.0 17.7 %gather_fusion.1 = f32[5120,4]{1,0:T(8,128)} fusion(f32[4,1024]{0,1:T(8,128)S(1)} %bitcast.877, s32[5120]{0:T(1024)S(1)} %get-tuple-element.802), kind=kCustom, calls=%fused_computation.1 | custom fusion | bytes 184320 | tf_op jit(solution)/shard_map/gather | solution.py:236
  30.2 3.8 collective-permute-start.9
  44.7 4.0 collective-permute-start.11
  51.9 28.2 %scatter_custom_fusion.1 = f32[4,1024]{0,1:T(8,128)S(1)} fusion(s32[5120]{0:T(1024)S(1)} %bitcast.1067, f32[5120,4]{1,0:T(8,128)} %copy.571, f32[]{:T(128)} %constant.674.clone.1), kind=kCustom, calls=%fused_computation.347 | custom fusion | flops 20480 | bytes 16896 | tf_op jit(solution)/shard_map/scatter-add | solution.py:247
  80.3 5.2 collective-permute-start.13
  97.2 9.0 collective-permute-start.15
  109.0 42.0 %gather_fusion = f32[5120]{0:T(1024)} fusion(f32[1024]{0:T(1024)S(1)} %bitcast.859, s32[5120]{0:T(1024)S(1)} %get-tuple-element.803), kind=kCustom, calls=%fused_computation | custom fusion | bytes 61440 | tf_op jit(solution)/shard_map/gather | solution.py:235
  154.6 3.6 fusion.225
  163.1 20.7 %gather_fusion.4 = f32[5120]{0:T(1024)S(1)} fusion(f32[1024]{0:T(1024)S(1)} %bitcast.860, s32[5120]{0:T(1024)S(1)} %get-tuple-element.803), kind=kCustom, calls=%fused_computation.4 | custom fusion | bytes 61440 | tf_op jit(solution)/shard_map/gather | solution.py:235
  184.0 7.8 collective-permute-start
  208.4 3.6 collective-permute-start.3
  214.4 3.4 collective-permute-start.19
  220.1 36.0 %scatter_custom_fusion = f32[1024]{0:T(1024)S(1)} fusion(s32[5120]{0:T(1024)} %bitcast.1071, f32[5120]{0:T(1024)S(1)} %bitcast.1124, f32[]{:T(128)} %constant.674.clone.1), kind=kCustom, calls=%fused_computation.673 | custom fusion | flops 5120 | bytes 4608 | tf_op jit(solution)/shard_map/scatter-add | solution.py:242
  258.3 3.5 collective-permute-start.4
  262.1 36.0 %scatter_custom_fusion.2 = f32[1024]{0:T(1024)S(1)} fusion(s32[5120]{0:T(1024)} %bitcast.1072, f32[5120]{0:T(1024)S(1)} %bitcast.1125, f32[]{:T(128)} %constant.674.clone.1), kind=kCustom, calls=%fused_computation.671 | custom fusion | flops 5120 | bytes 4608 | tf_op jit(solution)/shard_map/scatter-add | solution.py:242
  302.3 6.2 collective-permute-start.7
  313.8 8.6 collective-permute-start.21
  324.6 17.7 %gather_fusion.5 = f32[5120,4]{1,0:T(8,128)} fusion(f32[4,1024]{0,1:T(8,128)S(1)} %copy.587, s32[5120]{0:T(1024)S(1)} %get-tuple-element.802), kind=kCustom, calls=%fused_computation.5 | custom fusion | bytes 184320 | tf_op jit(solution)/shard_map/gather | solution.py:236
  353.0 7.9 collective-permute-start.23
  361.3 7.6 collective-permute-start.27
  368.9 4.3 collective-permute-start.26
  392.9 28.2 %scatter_custom_fusion.3 = f32[4,1024]{0,1:T(8,128)S(1)} fusion(s32[5120]{0:T(1024)} %bitcast.1068, f32[5120,4]{1,0:T(8,128)} %copy.589, f32[]{:T(128)} %constant.674.clone.1), kind=kCustom, calls=%fused_computation.345 | custom fusion | flops 20480 | bytes 16896 | tf_op jit(solution)/shard_map/scatter-add | solution.py:247
  428.4 6.3 collective-permute-start.35
  435.6 20.7 %gather_fusion.9 = f32[5120]{0:T(1024)S(1)} fusion(f32[1024]{0:T(1024)S(1)} %slice_bitcast_fusion.29, s32[5120]{0:T(1024)S(1)} %get-tuple-element.802), kind=kCustom, calls=%fused_computation.9 | custom fusion | bytes 61440 | tf_op jit(solution)/shard_map/gather | solution.py:279
  456.3 13.9 %collective-permute-start.51 = (f32[1,1024]{1,0:T(1,128)S(1)}, f32[1,1024]{1,0:T(1,128)S(1)}, u32[]{:S(2)}, u32[]{:S(2)}) collective-permute-start(f32[1,1024]{1,0:T(1,128)S(1)} %get-tuple-element.731), channel_id=1, source_target_pairs={{2,0},{3,1},{4,2},{5,3},{6,4},{7,5},{8,6},{9,7},{10,8},{11,9},{12,... | collective-permute-start | bytes 12296 | tf_op jit(solution)/shard_map/ppermute | solution.py:15
  472.2 3.6 collective-permute-start.28
  479.4 3.6 collective-permute-start.49
  486.6 7.8 collective-permute-done.48
  507.4 36.6 %scatter_custom_fusion.7 = f32[1024]{0:T(1024)} fusion(s32[5120]{0:T(1024)} %bitcast.1069, f32[5120]{0:T(1024)S(1)} %select_multiply_fusion.1, f32[]{:T(128)} %constant.674.clone.1), kind=kCustom, calls=%fused_computation.669 | custom fusion | flops 5120 | bytes 4608 | tf_op jit(solution)/shard_map/scatter-add | solution.py:285
  587.1 7.6 collective-permute-start.37
  608.5 3.5 scatter_custom_fusion.5
  614.1 8.4 collective-permute-start.39
  649.3 9.3 collective-permute-start.53
  658.7 19.4 %gather_fusion.8 = f32[5120,4]{1,0:T(8,128)} fusion(f32[4,1024]{0,1:T(8,128)S(1)} %copy.630, s32[5120]{0:T(1024)} %copy-done.32), kind=kCustom, calls=%fused_computation.8 | custom fusion | bytes 184320 | tf_op jit(solution)/shard_map/gather | solution.py:278
  692.5 3.5 scatter_custom_fusion.9
  698.1 7.9 collective-permute-start.55
  707.8 17.7 %gather_fusion.11 = f32[5120,4]{1,0:T(8,128)} fusion(f32[4,1024]{0,1:T(8,128)S(1)} %copy.663, s32[5120]{0:T(1024)S(1)} %copy-done.33), kind=kCustom, calls=%fused_computation.11 | custom fusion | bytes 184320 | tf_op jit(solution)/shard_map/gather | solution.py:278
  728.1 14.4 %collective-permute-start.40 = (f32[4,1024]{1,0:T(4,128)S(1)}, f32[4,1024]{1,0:T(4,128)S(1)}, u32[]{:S(2)}, u32[]{:S(2)}) collective-permute-start(f32[4,1024]{1,0:T(4,128)S(1)} %get-tuple-element.693), channel_id=1, source_target_pairs={{2,0},{3,1},{4,2},{5,3},{6,4},{7,5},{8,6},{9,7},{10,8},{11,9},{12,... | collective-permute-start | bytes 49160 | tf_op jit(solution)/shard_map/ppermute | solution.py:15
  762.4 3.7 collective-permute-done.63
  768.4 28.5 %scatter_custom_fusion.11 = f32[4,1024]{0,1:T(8,128)S(1)} fusion(s32[5120]{0:T(1024)} %bitcast.1073, f32[5120,4]{1,0:T(8,128)} %copy.665, f32[]{:T(128)} %constant.674.clone.1), kind=kCustom, calls=%fused_computation.341 | custom fusion | flops 20480 | bytes 16896 | tf_op jit(solution)/shard_map/scatter-add | solution.py:290
  800.0 28.2 %scatter_custom_fusion.6 = f32[4,1024]{0,1:T(8,128)S(1)} fusion(s32[5120]{0:T(1024)} %bitcast.1074, f32[5120,4]{1,0:T(8,128)} %copy.632, f32[]{:T(128)} %constant.674.clone.1), kind=kCustom, calls=%fused_computation.343 | custom fusion | flops 20480 | bytes 16896 | tf_op jit(solution)/shard_map/scatter-add | solution.py:290
  838.1 4.9 collective-permute-start.45
  846.3 74.6 %all-reduce.169 = (f32[64,81]{1,0:T(8,128)S(1)}, f32[64,9]{0,1:T(8,128)S(1)}, f32[12,64]{1,0:T(8,128)S(1)}, f32[64,9]{0,1:T(8,128)S(1)}, f32[48,64]{1,0:T(8,128)S(1)}) all-reduce(f32[64,81]{1,0:T(8,128)S(1)} %fusion.51, f32[64,9]{0,1:T(8,128)S(1)} %add_add_fusion.11, ...), channel_id=1, replica_groups=mesh['tile'=128] {'tile'}, use_global_device_ids=true, to_apply=%region_28.29 | all-reduce | flops 10176 | bytes 81408 | tf_op jit(solution)/shard_map/psum | solution.py:296
  931.5 20.7 %gather_fusion.10 = f32[5120]{0:T(1024)S(1)} fusion(f32[1024]{0:T(1024)S(1)} %slice_bitcast_fusion.24, s32[5120]{0:T(1024)S(1)} %copy-done.31), kind=kCustom, calls=%fused_computation.10 | custom fusion | bytes 61440 | tf_op jit(solution)/shard_map/gather | solution.py:279
  952.3 12.0 %collective-permute-start.59 = (f32[1,1024]{1,0:T(1,128)S(1)}, f32[1,1024]{1,0:T(1,128)S(1)}, u32[]{:S(2)}, u32[]{:S(2)}) collective-permute-start(f32[1,1024]{1,0:T(1,128)S(1)} %get-tuple-element.726), channel_id=1, source_target_pairs={{2,0},{3,1},{4,2},{5,3},{6,4},{7,5},{8,6},{9,7},{10,8},{11,9},{12,... | collective-permute-start | bytes 12296 | tf_op jit(solution)/shard_map/ppermute | solution.py:15
  966.2 3.6 collective-permute-start.57
  972.5 6.0 collective-permute-done.56
  978.5 36.0 %scatter_custom_fusion.10 = f32[1024]{0:T(1024)S(1)} fusion(s32[5120]{0:T(1024)} %bitcast.1070, f32[5120]{0:T(1024)S(1)} %select_multiply_fusion, f32[]{:T(128)} %constant.674.clone.1), kind=kCustom, calls=%fused_computation.667 | custom fusion | flops 5120 | bytes 4608 | tf_op jit(solution)/shard_map/scatter-add | solution.py:285
  (1157 shorter events, 302.1 us)
Async XLA Ops:
  7.3 1008.2 %all-reduce.173.cloned.1.call-start = ((), (), s32[]{:S(2)}) async-start(), calls=%async_computation | async-start | bytes 786432 | tf_op jit(solution)/shard_map/psum | solution.py:296
  30.2 12.5 %collective-permute-start.9 = (f32[4,1024]{1,0:T(4,128)S(1)}, f32[4,1024]{1,0:T(4,128)S(1)}, u32[]{:S(2)}, u32[]{:S(2)}) collective-permute-start(f32[4,1024]{1,0:T(4,128)S(1)} %get-tuple-element.702), channel_id=1, source_target_pairs={{0,1},{1,2},{2,3},{3,4},{4,5},{5,6},{6,7},{7,8},{8,9},{9,10},{10,1... | collective-permute-start | bytes 49160 | tf_op jit(solution)/shard_map/ppermute | solution.py:15
  33.9 8.7 collective-permute-start.8
  80.3 8.8 collective-permute-start.13
  95.2 55.8 %collective-permute-start.14 = (bf16[64,1,512]{0,2,1:T(8,128)(2,1)S(1)}, bf16[64,1,512]{0,2,1:T(8,128)(2,1)S(1)}, u32[]{:S(2)}, u32[]{:S(2)}) collective-permute-start(bf16[64,1,512]{0,2,1:T(8,128)(2,1)S(1)} %get-tuple-element.616), channel_id=1, source_target_pairs={{0,1},{1,2},{2,3},{3,4},{4,5},{5,6},{6,7},{7,8},{8,9},{9,10},{10,1... | collective-permute-start | bytes 196616 | tf_op jit(solution)/shard_map/ppermute | solution.py:26
  97.2 53.8 %collective-permute-start.15 = (bf16[64,1,512]{0,2,1:T(8,128)(2,1)S(1)}, bf16[64,1,512]{0,2,1:T(8,128)(2,1)S(1)}, u32[]{:S(2)}, u32[]{:S(2)}) collective-permute-start(bf16[64,1,512]{0,2,1:T(8,128)(2,1)S(1)} %get-tuple-element.617), channel_id=1, source_target_pairs={{1,0},{2,1},{3,2},{4,3},{5,4},{6,5},{7,6},{8,7},{9,8},{10,9},{11,1... | collective-permute-start | bytes 196616 | tf_op jit(solution)/shard_map/ppermute | solution.py:28
  184.0 21.4 %collective-permute-start = (f32[1,1024]{1,0:T(1,128)S(1)}, f32[1,1024]{1,0:T(1,128)S(1)}, u32[]{:S(2)}, u32[]{:S(2)}) collective-permute-start(f32[1,1024]{1,0:T(1,128)S(1)} %get-tuple-element.758), channel_id=1, source_target_pairs={{2,0},{3,1},{4,2},{5,3},{6,4},{7,5},{8,6},{9,7},{10,8},{11,9},{12,... | collective-permute-start | bytes 12296 | tf_op jit(solution)/shard_map/ppermute | solution.py:15
  199.3 15.1 %collective-permute-start.17 = (f32[1,1024]{1,0:T(1,128)S(1)}, f32[1,1024]{1,0:T(1,128)S(1)}, u32[]{:S(2)}, u32[]{:S(2)}) collective-permute-start(f32[1,1024]{1,0:T(1,128)S(1)} %get-tuple-element.762), channel_id=1, source_target_pairs={{1,0},{2,1},{3,2},{4,3},{5,4},{6,5},{7,6},{8,7},{9,8},{10,9},{11,1... | collective-permute-start | bytes 12296 | tf_op jit(solution)/shard_map/ppermute | solution.py:15
  201.6 12.8 %collective-permute-start.16 = (f32[1,1024]{1,0:T(1,128)S(1)}, f32[1,1024]{1,0:T(1,128)S(1)}, u32[]{:S(2)}, u32[]{:S(2)}) collective-permute-start(f32[1,1024]{1,0:T(1,128)S(1)} %get-tuple-element.763), channel_id=1, source_target_pairs={{2,0},{3,1},{4,2},{5,3},{6,4},{7,5},{8,6},{9,7},{10,8},{11,9},{12,... | collective-permute-start | bytes 12296 | tf_op jit(solution)/shard_map/ppermute | solution.py:15
  208.4 11.6 %collective-permute-start.3 = (f32[1,1024]{1,0:T(1,128)S(1)}, f32[1,1024]{1,0:T(1,128)S(1)}, u32[]{:S(2)}, u32[]{:S(2)}) collective-permute-start(f32[1,1024]{1,0:T(1,128)S(1)} %get-tuple-element.754), channel_id=1, source_target_pairs={{0,2},{1,3},{2,4},{3,5},{4,6},{5,7},{6,8},{7,9},{8,10},{9,11},{10,... | collective-permute-start | bytes 12296 | tf_op jit(solution)/shard_map/ppermute | solution.py:15
  214.4 47.6 %collective-permute-start.19 = (f32[1,1024]{1,0:T(1,128)S(1)}, f32[1,1024]{1,0:T(1,128)S(1)}, u32[]{:S(2)}, u32[]{:S(2)}) collective-permute-start(f32[1,1024]{1,0:T(1,128)S(1)} %get-tuple-element.759), channel_id=1, source_target_pairs={{0,2},{1,3},{2,4},{3,5},{4,6},{5,7},{6,8},{7,9},{8,10},{9,11},{10,... | collective-permute-start | bytes 12296 | tf_op jit(solution)/shard_map/ppermute | solution.py:15
  217.8 44.1 %collective-permute-start.18 = (f32[1,1024]{1,0:T(1,128)S(1)}, f32[1,1024]{1,0:T(1,128)S(1)}, u32[]{:S(2)}, u32[]{:S(2)}) collective-permute-start(f32[1,1024]{1,0:T(1,128)S(1)} %get-tuple-element.760), channel_id=1, source_target_pairs={{0,1},{1,2},{2,3},{3,4},{4,5},{5,6},{6,7},{7,8},{8,9},{9,10},{10,1... | collective-permute-start | bytes 12296 | tf_op jit(solution)/shard_map/ppermute | solution.py:15
  256.3 41.8 %collective-permute-start.5 = (bf16[9,1,128]{2,0,1:T(8,128)(2,1)S(1)}, bf16[9,1,128]{2,0,1:T(8,128)(2,1)S(1)}, u32[]{:S(2)}, u32[]{:S(2)}) collective-permute-start(bf16[9,1,128]{2,0,1:T(8,128)(2,1)S(1)} %get-tuple-element.748), channel_id=1, source_target_pairs={{1,0},{2,1},{3,2},{4,3},{5,4},{6,5},{7,6},{8,7},{9,8},{10,9},{11,1... | collective-permute-start | bytes 6920 | tf_op jit(solution)/shard_map/ppermute | solution.py:28
  258.3 39.8 %collective-permute-start.4 = (bf16[9,1,128]{2,0,1:T(8,128)(2,1)S(1)}, bf16[9,1,128]{2,0,1:T(8,128)(2,1)S(1)}, u32[]{:S(2)}, u32[]{:S(2)}) collective-permute-start(bf16[9,1,128]{2,0,1:T(8,128)(2,1)S(1)} %get-tuple-element.749), channel_id=1, source_target_pairs={{0,1},{1,2},{2,3},{3,4},{4,5},{5,6},{6,7},{7,8},{8,9},{9,10},{10,1... | collective-permute-start | bytes 6920 | tf_op jit(solution)/shard_map/ppermute | solution.py:26
  300.4 8.2 collective-permute-start.6
  313.8 35.0 %collective-permute-start.21 = (bf16[9,1,128]{2,0,1:T(8,128)(2,1)S(1)}, bf16[9,1,128]{2,0,1:T(8,128)(2,1)S(1)}, u32[]{:S(2)}, u32[]{:S(2)}) collective-permute-start(bf16[9,1,128]{2,0,1:T(8,128)(2,1)S(1)} %get-tuple-element.740), channel_id=1, source_target_pairs={{1,0},{2,1},{3,2},{4,3},{5,4},{6,5},{7,6},{8,7},{9,8},{10,9},{11,1... | collective-permute-start | bytes 6920 | tf_op jit(solution)/shard_map/ppermute | solution.py:28
  322.4 26.4 %collective-permute-start.20 = (bf16[9,1,128]{2,0,1:T(8,128)(2,1)S(1)}, bf16[9,1,128]{2,0,1:T(8,128)(2,1)S(1)}, u32[]{:S(2)}, u32[]{:S(2)}) collective-permute-start(bf16[9,1,128]{2,0,1:T(8,128)(2,1)S(1)} %get-tuple-element.741), channel_id=1, source_target_pairs={{0,1},{1,2},{2,3},{3,4},{4,5},{5,6},{6,7},{7,8},{8,9},{9,10},{10,1... | collective-permute-start | bytes 6920 | tf_op jit(solution)/shard_map/ppermute | solution.py:26
  344.8 16.5 %collective-permute-start.25 = (f32[4,1024]{1,0:T(4,128)S(1)}, f32[4,1024]{1,0:T(4,128)S(1)}, u32[]{:S(2)}, u32[]{:S(2)}) collective-permute-start(f32[4,1024]{1,0:T(4,128)S(1)} %get-tuple-element.697), channel_id=1, source_target_pairs={{0,1},{1,2},{2,3},{3,4},{4,5},{5,6},{6,7},{7,8},{8,9},{9,10},{10,1... | collective-permute-start | bytes 49160 | tf_op jit(solution)/shard_map/ppermute | solution.py:15
  346.7 14.5 %collective-permute-start.24 = (f32[4,1024]{1,0:T(4,128)S(1)}, f32[4,1024]{1,0:T(4,128)S(1)}, u32[]{:S(2)}, u32[]{:S(2)}) collective-permute-start(f32[4,1024]{1,0:T(4,128)S(1)} %get-tuple-element.698), channel_id=1, source_target_pairs={{0,2},{1,3},{2,4},{3,5},{4,6},{5,7},{6,8},{7,9},{8,10},{9,11},{10,... | collective-permute-start | bytes 49160 | tf_op jit(solution)/shard_map/ppermute | solution.py:15
  351.1 22.2 %collective-permute-start.22 = (bf16[64,1,128]{2,1,0:T(2,128)(2,1)S(1)}, bf16[64,1,128]{2,1,0:T(2,128)(2,1)S(1)}, u32[]{:S(2)}, u32[]{:S(2)}) collective-permute-start(bf16[64,1,128]{2,1,0:T(2,128)(2,1)S(1)} %get-tuple-element.676), channel_id=1, source_target_pairs={{0,1},{1,2},{2,3},{3,4},{4,5},{5,6},{6,7},{7,8},{8,9},{9,10},{10,1... | collective-permute-start | bytes 49160 | tf_op jit(solution)/shard_map/ppermute | solution.py:26
  353.0 20.3 %collective-permute-start.23 = (bf16[64,1,128]{2,1,0:T(2,128)(2,1)S(1)}, bf16[64,1,128]{2,1,0:T(2,128)(2,1)S(1)}, u32[]{:S(2)}, u32[]{:S(2)}) collective-permute-start(bf16[64,1,128]{2,1,0:T(2,128)(2,1)S(1)} %get-tuple-element.677), channel_id=1, source_target_pairs={{1,0},{2,1},{3,2},{4,3},{5,4},{6,5},{7,6},{8,7},{9,8},{10,9},{11,1... | collective-permute-start | bytes 49160 | tf_op jit(solution)/shard_map/ppermute | solution.py:28
  361.3 29.3 %collective-permute-start.27 = (f32[4,1024]{1,0:T(4,128)S(1)}, f32[4,1024]{1,0:T(4,128)S(1)}, u32[]{:S(2)}, u32[]{:S(2)}) collective-permute-start(f32[4,1024]{1,0:T(4,128)S(1)} %get-tuple-element.694), channel_id=1, source_target_pairs={{2,0},{3,1},{4,2},{5,3},{6,4},{7,5},{8,6},{9,7},{10,8},{11,9},{12,... | collective-permute-start | bytes 49160 | tf_op jit(solution)/shard_map/ppermute | solution.py:15
  368.9 21.6 %collective-permute-start.26 = (f32[4,1024]{1,0:T(4,128)S(1)}, f32[4,1024]{1,0:T(4,128)S(1)}, u32[]{:S(2)}, u32[]{:S(2)}) collective-permute-start(f32[4,1024]{1,0:T(4,128)S(1)} %get-tuple-element.695), channel_id=1, source_target_pairs={{1,0},{2,1},{3,2},{4,3},{5,4},{6,5},{7,6},{8,7},{9,8},{10,9},{11,1... | collective-permute-start | bytes 49160 | tf_op jit(solution)/shard_map/ppermute | solution.py:15
  386.1 35.1 %collective-permute-start.32 = (bf16[64,1,128]{2,1,0:T(2,128)(2,1)}, bf16[64,1,128]{2,1,0:T(2,128)(2,1)}, u32[]{:S(2)}, u32[]{:S(2)}) collective-permute-start(bf16[64,1,128]{2,1,0:T(2,128)(2,1)} %get-tuple-element.608), channel_id=1, source_target_pairs={{0,1},{1,2},{2,3},{3,4},{4,5},{5,6},{6,7},{7,8},{8,9},{9,10},{10,1... | collective-permute-start | bytes 49160 | tf_op jit(solution)/shard_map/ppermute | solution.py:26
  388.1 33.2 %collective-permute-start.33 = (bf16[64,1,128]{2,1,0:T(2,128)(2,1)}, bf16[64,1,128]{2,1,0:T(2,128)(2,1)}, u32[]{:S(2)}, u32[]{:S(2)}) collective-permute-start(bf16[64,1,128]{2,1,0:T(2,128)(2,1)} %get-tuple-element.609), channel_id=1, source_target_pairs={{1,0},{2,1},{3,2},{4,3},{5,4},{6,5},{7,6},{8,7},{9,8},{10,9},{11,1... | collective-permute-start | bytes 49160 | tf_op jit(solution)/shard_map/ppermute | solution.py:28
  425.2 9.5 collective-permute-start.34
  456.3 26.7 %collective-permute-start.51 = (f32[1,1024]{1,0:T(1,128)S(1)}, f32[1,1024]{1,0:T(1,128)S(1)}, u32[]{:S(2)}, u32[]{:S(2)}) collective-permute-start(f32[1,1024]{1,0:T(1,128)S(1)} %get-tuple-element.731), channel_id=1, source_target_pairs={{2,0},{3,1},{4,2},{5,3},{6,4},{7,5},{8,6},{9,7},{10,8},{11,9},{12,... | collective-permute-start | bytes 12296 | tf_op jit(solution)/shard_map/ppermute | solution.py:15
  470.3 24.8 %collective-permute-start.29 = (bf16[52,1,512]{2,0,1:T(8,128)(2,1)S(1)}, bf16[52,1,512]{2,0,1:T(8,128)(2,1)S(1)}, u32[]{:S(2)}, u32[]{:S(2)}) collective-permute-start(bf16[52,1,512]{2,0,1:T(8,128)(2,1)S(1)} %get-tuple-element.681), channel_id=1, source_target_pairs={{1,0},{2,1},{3,2},{4,3},{5,4},{6,5},{7,6},{8,7},{9,8},{10,9},{11,1... | collective-permute-start | bytes 159752 | tf_op jit(solution)/shard_map/ppermute | solution.py:28
  472.2 22.9 %collective-permute-start.28 = (bf16[52,1,512]{2,0,1:T(8,128)(2,1)S(1)}, bf16[52,1,512]{2,0,1:T(8,128)(2,1)S(1)}, u32[]{:S(2)}, u32[]{:S(2)}) collective-permute-start(bf16[52,1,512]{2,0,1:T(8,128)(2,1)S(1)} %get-tuple-element.680), channel_id=1, source_target_pairs={{0,1},{1,2},{2,3},{3,4},{4,5},{5,6},{6,7},{7,8},{8,9},{9,10},{10,1... | collective-permute-start | bytes 159752 | tf_op jit(solution)/shard_map/ppermute | solution.py:26
  477.5 8.3 collective-permute-start.50
  483.0 11.3 %collective-permute-start.48 = (f32[1,1024]{1,0:T(1,128)S(1)}, f32[1,1024]{1,0:T(1,128)S(1)}, u32[]{:S(2)}, u32[]{:S(2)}) collective-permute-start(f32[1,1024]{1,0:T(1,128)S(1)} %get-tuple-element.735), channel_id=1, source_target_pairs={{0,2},{1,3},{2,4},{3,5},{4,6},{5,7},{6,8},{7,9},{8,10},{9,11},{10,... | collective-permute-start | bytes 12296 | tf_op jit(solution)/shard_map/ppermute | solution.py:15
  502.3 41.7 %collective-permute-start.30 = (bf16[64,1,512]{0,2,1:T(8,128)(2,1)S(1)}, bf16[64,1,512]{0,2,1:T(8,128)(2,1)S(1)}, u32[]{:S(2)}, u32[]{:S(2)}) collective-permute-start(bf16[64,1,512]{0,2,1:T(8,128)(2,1)S(1)} %get-tuple-element.614), channel_id=1, source_target_pairs={{0,1},{1,2},{2,3},{3,4},{4,5},{5,6},{6,7},{7,8},{8,9},{9,10},{10,1... | collective-permute-start | bytes 196616 | tf_op jit(solution)/shard_map/ppermute | solution.py:26
  504.2 39.8 %collective-permute-start.31 = (bf16[64,1,512]{0,2,1:T(8,128)(2,1)S(1)}, bf16[64,1,512]{0,2,1:T(8,128)(2,1)S(1)}, u32[]{:S(2)}, u32[]{:S(2)}) collective-permute-start(bf16[64,1,512]{0,2,1:T(8,128)(2,1)S(1)} %get-tuple-element.615), channel_id=1, source_target_pairs={{1,0},{2,1},{3,2},{4,3},{5,4},{6,5},{7,6},{8,7},{9,8},{10,9},{11,1... | collective-permute-start | bytes 196616 | tf_op jit(solution)/shard_map/ppermute | solution.py:28
  584.7 11.7 %collective-permute-start.36 = (bf16[64,1,512]{0,2,1:T(8,128)(2,1)S(1)}, bf16[64,1,512]{0,2,1:T(8,128)(2,1)S(1)}, u32[]{:S(2)}, u32[]{:S(2)}) collective-permute-start(bf16[64,1,512]{0,2,1:T(8,128)(2,1)S(1)} %get-tuple-element.555), channel_id=1, source_target_pairs={{0,1},{1,2},{2,3},{3,4},{4,5},{5,6},{6,7},{7,8},{8,9},{9,10},{10,1... | collective-permute-start | bytes 196616 | tf_op jit(solution)/shard_map/ppermute | solution.py:26
  587.1 9.3 collective-permute-start.37
  612.2 10.4 %collective-permute-start.38 = (bf16[52,1,512]{2,0,1:T(8,128)(2,1)S(1)}, bf16[52,1,512]{2,0,1:T(8,128)(2,1)S(1)}, u32[]{:S(2)}, u32[]{:S(2)}) collective-permute-start(bf16[52,1,512]{2,0,1:T(8,128)(2,1)S(1)} %get-tuple-element.624), channel_id=1, source_target_pairs={{0,1},{1,2},{2,3},{3,4},{4,5},{5,6},{6,7},{7,8},{8,9},{9,10},{10,1... | collective-permute-start | bytes 159752 | tf_op jit(solution)/shard_map/ppermute | solution.py:26
  614.1 9.3 collective-permute-start.39
  647.4 34.1 %collective-permute-start.52 = (bf16[64,1,512]{0,2,1:T(8,128)(2,1)S(1)}, bf16[64,1,512]{0,2,1:T(8,128)(2,1)}, u32[]{:S(2)}, u32[]{:S(2)}) collective-permute-start(bf16[64,1,512]{0,2,1:T(8,128)(2,1)S(1)} %get-tuple-element.544), channel_id=1, source_target_pairs={{0,1},{1,2},{2,3},{3,4},{4,5},{5,6},{6,7},{7,8},{8,9},{9,10},{10,1... | collective-permute-start | bytes 196616 | tf_op jit(solution)/shard_map/ppermute | solution.py:26
  649.3 32.2 %collective-permute-start.53 = (bf16[64,1,512]{0,2,1:T(8,128)(2,1)}, bf16[64,1,512]{0,2,1:T(8,128)(2,1)}, u32[]{:S(2)}, u32[]{:S(2)}) collective-permute-start(bf16[64,1,512]{0,2,1:T(8,128)(2,1)} %get-tuple-element.545), channel_id=1, source_target_pairs={{1,0},{2,1},{3,2},{4,3},{5,4},{6,5},{7,6},{8,7},{9,8},{10,9},{11,1... | collective-permute-start | bytes 196616 | tf_op jit(solution)/shard_map/ppermute | solution.py:28
  696.1 9.9 collective-permute-start.54
  698.1 8.8 collective-permute-start.55
  728.1 20.6 %collective-permute-start.40 = (f32[4,1024]{1,0:T(4,128)S(1)}, f32[4,1024]{1,0:T(4,128)S(1)}, u32[]{:S(2)}, u32[]{:S(2)}) collective-permute-start(f32[4,1024]{1,0:T(4,128)S(1)} %get-tuple-element.693), channel_id=1, source_target_pairs={{2,0},{3,1},{4,2},{5,3},{6,4},{7,5},{8,6},{9,7},{10,8},{11,9},{12,... | collective-permute-start | bytes 49160 | tf_op jit(solution)/shard_map/ppermute | solution.py:15
  742.5 14.8 %collective-permute-start.61 = (f32[4,1024]{1,0:T(4,128)S(1)}, f32[4,1024]{1,0:T(4,128)S(1)}, u32[]{:S(2)}, u32[]{:S(2)}) collective-permute-start(f32[4,1024]{1,0:T(4,128)S(1)} %get-tuple-element.687), channel_id=1, source_target_pairs={{1,0},{2,1},{3,2},{4,3},{5,4},{6,5},{7,6},{8,7},{9,8},{10,9},{11,1... | collective-permute-start | bytes 49160 | tf_op jit(solution)/shard_map/ppermute | solution.py:15
  744.4 12.9 %collective-permute-start.60 = (f32[4,1024]{1,0:T(4,128)S(1)}, f32[4,1024]{1,0:T(4,128)S(1)}, u32[]{:S(2)}, u32[]{:S(2)}) collective-permute-start(f32[4,1024]{1,0:T(4,128)S(1)} %get-tuple-element.688), channel_id=1, source_target_pairs={{2,0},{3,1},{4,2},{5,3},{6,4},{7,5},{8,6},{9,7},{10,8},{11,9},{12,... | collective-permute-start | bytes 49160 | tf_op jit(solution)/shard_map/ppermute | solution.py:15
  751.7 46.0 %collective-permute-start.43 = (f32[4,1024]{1,0:T(4,128)S(1)}, f32[4,1024]{1,0:T(4,128)S(1)}, u32[]{:S(2)}, u32[]{:S(2)}) collective-permute-start(f32[4,1024]{1,0:T(4,128)S(1)} %get-tuple-element.689), channel_id=1, source_target_pairs={{0,2},{1,3},{2,4},{3,5},{4,6},{5,7},{6,8},{7,9},{8,10},{9,11},{10,... | collective-permute-start | bytes 49160 | tf_op jit(solution)/shard_map/ppermute | solution.py:15
  757.4 8.7 collective-permute-start.63
  952.3 20.2 %collective-permute-start.59 = (f32[1,1024]{1,0:T(1,128)S(1)}, f32[1,1024]{1,0:T(1,128)S(1)}, u32[]{:S(2)}, u32[]{:S(2)}) collective-permute-start(f32[1,1024]{1,0:T(1,128)S(1)} %get-tuple-element.726), channel_id=1, source_target_pairs={{2,0},{3,1},{4,2},{5,3},{6,4},{7,5},{8,6},{9,7},{10,8},{11,9},{12,... | collective-permute-start | bytes 12296 | tf_op jit(solution)/shard_map/ppermute | solution.py:15
  969.9 8.6 collective-permute-start.56
  (256 other events, 4159.9 us)
Sparse Core Ops, SparseCore 0:
  843.2 147.3 all-reduce.172
where the time goes:
time: 1040 us; the launch traced here: 1030 us
  other arithmetic  330 us (32%)
  local copies, waits for them, and re-layouts  285 us (27%)
  starting transfers between devices  255 us (25%)
  blocking collectives  74.6 us (7%)
  waiting for transfers between devices  37.5 us (4%)
  matrix products  27.2 us (3%)
  between operations  20.4 us (2%)
    ppermute x32, starting transfers between devices, passed_along(): return lax.ppermute(shard, axis, pairs)  125 us
    ppermute x16, starting transfers between devices, with_halo(): lax.ppermute(head, axis, [((i + 1) % count, i) for i in range(ends)])  93.4 us
    psum x1, blocking collectives, body(): summed = lax.psum(air_total + sea_total, 'tile')  74.6 us
    scatter-add x2, other arithmetic, body(): interface_transfer_map = jnp.zeros((sea_rows * sea_cols,), jnp.float32).a...  72.6 us
    scatter-add x2, other arithmetic, body(): skin_heat_level = jnp.zeros((air_latitude_total * air_longitude_total,),...  72 us
    gather x2, local copies, waits for them, and re-layouts, body(): surface_flat[sea_slots]  62.8 us
    scatter-add x2, other arithmetic, body(): fluxes = jnp.zeros((flux_channels, air_latitude_total * air_longitude_tot...  56.6 us
    scatter-add x2, other arithmetic, body(): inbound_energy_map = jnp.zeros((flux_channels, sea_rows * sea_cols), jnp....  56.4 us
  transfers between devices with their start and end apart: 65, of which 17 were waited for; matrix products, arithmetic and copies ran while one was open for 34% of the time, Pallas kernels for 0%

commit v1 on v0

v1 whole, which is shorter than its diff:
```python
import math

import jax
import jax.numpy as jnp
from jax import lax
from jax.experimental import pallas as pl
from jax.experimental.pallas import tpu as pltpu
from jax.sharding import PartitionSpec as P

MESH = pl.DeviceIdType.MESH
F32 = jnp.float32
BF = jnp.bfloat16
OFFS = (-2, -1, 1, 2)
NEAR = 5
SL = 1024
C0 = math.sqrt(2.0 / math.pi)
C1 = 0.044715


def nn(a, b):
    return jnp.dot(a, b, preferred_element_type=F32)


def nt(a, b):
    return lax.dot_general(a, b, (((1,), (1,)), ((), ())), preferred_element_type=F32)


def tn(a, b):
    return lax.dot_general(a, b, (((0,), (0,)), ((), ())), preferred_element_type=F32)


def roll(x, by):
    return pltpu.roll(x, by % x.shape[1], axis=1)


class Names:
    def __init__(self, names, refs):
        for name, ref in zip(names, refs):
            setattr(self, name, ref)


class Model:
    def __init__(self, name, rows, width, state, inputs, chans, given, outs):
        self.name, self.rows, self.width = name, rows, width
        self.state, self.chans, self.outs = state, chans, outs
        self.inputs, self.given = inputs, given
        self.ext = (rows + 4) * width
        self.pad = (rows + 2) * width

    def scratch(self):
        f, b = F32, BF
        n, kc = self.name, self.chans
        return [
            (n + "_x", (kc, self.ext), f),
            (n + "_s3", (2, 3 * kc, self.ext), b),
            (n + "_y", (192, self.ext), f),
            (n + "_fp", (2, 64, self.pad), f),
            (n + "_mix", (64, SL), f),
            (n + "_nrm", (2, 64, SL), f),
            (n + "_rstd", (2, 1, SL), f),
            (n + "_dgelu", (2, 256, SL), f),
            (n + "_hid", (2, 256, SL), b),
            (n + "_resb", (2, 64, SL), b),
            (n + "_out", (self.outs, SL), f),
            (n + "_cot", (self.outs, SL), f),
            (n + "_dyb", (self.outs, SL), b),
            (n + "_dresb", (64, SL), b),
            (n + "_dpreb", (256, SL), b),
            (n + "_dmr", (3, 64, SL), f),
            (n + "_dfs", (192, self.ext), b),
            (n + "_ds3", (3 * kc, self.ext), f),
            (n + "_dx", (kc, self.ext), f),
            (n + "_encf", (192, 3 * kc), f),
            (n + "_enc", (192, 3 * kc), b),
            (n + "_enct", (3 * kc, 192), b),
            (n + "_exp", (256, 64), b),
            (n + "_cont", (256, 64), b),
            (n + "_decf", (self.outs, 64), f),
            (n + "_dec", (self.outs, 64), b),
            (n + "_dect", (64, self.outs), b),
            (n + "_dw", (64, 16), f),
        ]


AIR = Model("air", 8, 128, 8, 9, 16, 12, 16)
SEA = Model("sea", 2, 512, 48, 52, 64, 48, 48)

INPUTS = (
    "air_state",
    "sea_state",
    "flux",
    "air_cells",
    "sea_cells",
    "counts",
    "sea_share",
    "air_share",
    "partner",
    "wet",
    "air_c",
    "sea_c",
    "air_renc",
    "air_rdw",
    "air_expt",
    "air_con",
    "air_rdec",
    "sea_renc",
    "sea_rdw",
    "sea_expt",
    "sea_con",
    "sea_rdec",
)
OUTPUTS = ("o_air", "o_sea", "o_dair", "o_dsea", "o_dflux", "o_grads")
WEIGHTS = ("enc", "dw", "exp", "con", "dec")

COPIES = 80
GROWS = 1024
G_EXP, G_CON, G_ENC0, G_ENC1, G_DEC, G_DW = 0, 256, 512, 704, 896, 960


def scratch_list():
    f, b = F32, BF
    items = AIR.scratch() + SEA.scratch()
    items += [
        ("meta_pay", (4, 8, SL), f),
        ("meta_in", (NEAR, 8, SL), f),
        ("oh_aa", (128, NEAR * SL), b),
        ("oh_as", (128, NEAR * SL), b),
        ("oh_sa", (128, NEAR * SL), b),
        ("oh_ss", (128, NEAR * SL), b),
        ("fold", (512, 512), b),
        ("wetf", (1, SL), f),
        ("a_now", (8, SL), f),
        ("o_now", (48, SL), f),
        ("pay_f", (2, 32, 128), f),
        ("in_f", (2, 4, 32, 128), f),
        ("pay_s", (2, 8, 128), f),
        ("in_s", (2, 4, 8, 128), f),
        ("halo_s", (2, 48, SL), b),
        ("halo_s_in", (2, 2, 48, SL), b),
        ("halo_a", (2, 2, 8, 256), f),
        ("halo_a_in", (2, 2, 8, 256), f),
        ("pay_g", (2, 32, 128), f),
        ("in_g", (2, 2, 32, 128), f),
        ("pay_k", (2, 8, 128), f),
        ("in_k", (2, 2, 8, 128), f),
        ("ret_s", (2, 2, 48, SL), b),
        ("ret_s_in", (2, 2, 48, SL), b),
        ("ret_g", (2, 2, 8, SL), f),
        ("ret_g_in", (2, 2, 8, SL), f),
        ("ret_a", (2, 2, 16, 256), f),
        ("ret_a_in", (2, 2, 16, 256), f),
        ("pay_dg", (2, 32, 128), f),
        ("in_dg", (2, 4, 32, 128), f),
        ("pay_dk", (2, 8, 128), f),
        ("in_dk", (2, 4, 8, 128), f),
        ("tmp32", (32, 128), f),
        ("tmp8", (8, 128), f),
        ("g32", (GROWS, 128), f),
        ("gb", (2, 4, 8, 16, 128), b),
        ("r1", (4, 8, 16, 128), b),
        ("h1", (4, 8, 16, 128), b),
        ("r2", (3, 8, 16, 128), b),
        ("h2", (8, 16, 128), b),
        ("r3", (4, 8, 16, 128), b),
        ("h3", (8, 16, 128), b),
        ("r4", (4, 8, 16, 128), b),
        ("gout", (2, 4, 8, 16, 128), b),
    ]
    return items


def kernel(n, *refs):
    names = INPUTS + OUTPUTS + tuple(item[0] for item in scratch_list()) + ("ssem", "rsem")
    r = Names(names, refs)
    me = lax.axis_index("tile")
    core = lax.rem(me, 2)
    yy = lax.rem(me // 2, 4)
    nx = min(4, n // 8)
    nz = n // (8 * nx)
    xx = lax.rem(me // 8, nx)
    zz = me // (8 * nx)
    first = me == 0
    last = me == n - 1
    low_on = jnp.where(first, 0.0, 1.0).astype(F32)
    up_on = jnp.where(last, 0.0, 1.0).astype(F32)
    last_f = 1.0 - up_on

    def near(off):
        return lax.rem(me + (off + n), n)

    def at(z, x, y, c):
        return ((z * nx + x) * 4 + y) * 2 + c

    peer_core = at(zz, xx, yy, 1 - core)
    peers_y = [at(zz, xx, lax.rem(yy + s, 4), core) for s in (1, 2, 3)]
    peers_x = [at(zz, lax.rem(xx + s, nx), yy, core) for s in range(1, nx)]
    peers_z = [at(lax.rem(zz + s, nz), xx, yy, core) for s in range(1, nz)]

    count = [0]

    def send(src, dst, dev):
        i = count[0]
        count[0] += 1
        copy = pltpu.make_async_remote_copy(
            src_ref=src,
            dst_ref=dst,
            send_sem=r.ssem.at[i],
            recv_sem=r.rsem.at[i],
            device_id=(dev,),
            device_id_type=MESH,
        )
        copy.start()
        return copy

    def wait(copies):
        for copy in copies:
            copy.wait()

    iota8 = lax.broadcasted_iota(jnp.int32, (8, SL), 0)
    iota32 = lax.broadcasted_iota(jnp.int32, (32, SL), 0) // 4

    everyone = [near(off) for off in OFFS] + peers_y + peers_x + peers_z
    barrier = pltpu.get_barrier_semaphore()
    for dev in everyone:
        pl.semaphore_signal(barrier, inc=1, device_id=(dev,), device_id_type=MESH)

    lane = lax.broadcasted_iota(jnp.int32, (1, SL), 1)

    def meta_rows(k_out, k_air, ref, i):
        used = lane < r.counts[0:1, k_out : k_out + 1]
        ref[i, 0:1, :] = r.sea_cells[k_out].astype(F32)
        ref[i, 1:2, :] = jnp.where(used, r.air_share[k_out], 0.0)
        ref[i, 2:3, :] = jnp.where(used, r.sea_share[k_out], 0.0)
        ref[i, 3:4, :] = r.air_cells[k_air].astype(F32)

    r.meta_pay[...] = jnp.zeros_like(r.meta_pay)
    for i, off in enumerate(OFFS):
        meta_rows(off + 2, 2 - off, r.meta_pay, i)

    for row in range(8):
        lanes = slice(row * 128, (row + 1) * 128)
        r.a_now[:, lanes] = r.air_state[:, row, :]
        r.air_cot[0:8, lanes] = r.air_c[:, row, :]
        r.pay_f[0, row * 4 : row * 4 + 4, :] = r.flux[:, row, :]
    r.air_cot[8:16, :] = jnp.zeros((8, SL), F32)
    for row in range(2):
        lanes = slice(row * 512, (row + 1) * 512)
        r.o_now[:, lanes] = r.sea_state[:, row, :]
        r.sea_cot[:, lanes] = r.sea_c[:, row, :]
        r.wetf[:, lanes] = r.wet[row : row + 1, :].astype(F32)

    def start_f(step):
        return [send(r.pay_f.at[step], r.in_f.at[step, i], near(off)) for i, off in enumerate(OFFS)]

    def start_s(step):
        for hi in range(8):
            r.pay_s[step, hi : hi + 1, :] = r.o_now[0:1, hi * 128 : (hi + 1) * 128]
        return [send(r.pay_s.at[step], r.in_s.at[step, i], near(off)) for i, off in enumerate(OFFS)]

    def start_halo_sea(step):
        r.halo_s[step] = r.o_now[...].astype(BF)
        return [
            send(r.halo_s.at[step], r.halo_s_in.at[step, i], near(off))
            for i, off in enumerate((-1, 1))
        ]

    def start_halo_air(step):
        r.halo_a[step, 0] = r.a_now[:, 0:256]
        r.halo_a[step, 1] = r.a_now[:, SL - 256 : SL]
        return [
            send(r.halo_a.at[step, i], r.halo_a_in.at[step, i], near(off))
            for i, off in enumerate((-1, 1))
        ]

    pl.semaphore_wait(barrier, len(everyone))
    metas = [
        send(r.meta_pay.at[i], r.meta_in.at[off + 2], near(off)) for i, off in enumerate(OFFS)
    ]
    sent_s, sent_f = start_s(0), start_f(0)
    halo_air, halo_sea = start_halo_air(0), start_halo_sea(0)
    meta_rows(2, 2, r.meta_in, 2)

    r.g32[...] = jnp.zeros_like(r.g32)
    for m in (AIR, SEA):
        x = getattr(r, m.name + "_x")
        x[m.state : m.chans, :] = jnp.zeros((m.chans - m.state, m.ext), F32)
        dfs = getattr(r, m.name + "_dfs")
        dfs[...] = jnp.zeros_like(dfs)
        g = lambda s: getattr(r, m.name + "_" + s)
        kc, chans = m.chans, m.inputs
        g("encf")[...] = jnp.zeros_like(g("encf"))
        raw = g("renc")[...].astype(F32)
        for i in range(3):
            for j in range(3):
                t = 3 * i + j
                g("encf")[i * 64 : (i + 1) * 64, j * kc : j * kc + chans] = raw[:, t * chans : (t + 1) * chans]
        enc = g("encf")[...]
        g("enc")[...] = enc.astype(BF)
        g("enct")[...] = jnp.transpose(enc).astype(BF)
        g("exp")[...] = jnp.transpose(g("expt")[...].astype(F32)).astype(BF)
        g("cont")[...] = jnp.transpose(g("con")[...].astype(F32)).astype(BF)
        g("decf")[...] = jnp.zeros_like(g("decf"))
        g("decf")[0 : m.given, :] = g("rdec")[...].astype(F32)
        dec = g("decf")[...]
        g("dec")[...] = dec.astype(BF)
        g("dect")[...] = jnp.transpose(dec).astype(BF)
        taps = jnp.concatenate([g("rdw")[...].astype(F32), jnp.zeros((7, 64), F32)], axis=0)
        g("dw")[...] = jnp.transpose(taps)
    source = lax.broadcasted_iota(jnp.int32, (512, 512), 0)
    r.fold[...] = jnp.where(source == r.partner[...], 1.0, 0.0).astype(BF)
    iota128 = lax.broadcasted_iota(jnp.int32, (128, SL), 0)

    def one_hot(row):
        low = jnp.bitwise_and(row, 127)
        return jnp.where(iota128 == low, 1.0, 0.0).astype(BF)

    for k in range(NEAR):
        lanes = slice(k * SL, (k + 1) * SL)
        r.oh_aa[:, lanes] = one_hot(r.air_cells[k])
        r.oh_ss[:, lanes] = one_hot(r.sea_cells[k])

    def air_meta(k, row):
        return r.meta_in[k, row : row + 1, :]

    def sea_meta(k, row):
        return r.meta_in[4 - k, row : row + 1, :]

    def own_weight(k, row):
        share = r.air_share if row == 1 else r.sea_share
        used = lane < r.counts[0:1, k : k + 1]
        return jnp.where(used, share[k], 0.0)

    wait(metas)
    for k in range(NEAR):
        lanes = slice(k * SL, (k + 1) * SL)
        r.oh_as[:, lanes] = one_hot(air_meta(k, 0).astype(jnp.int32))
        r.oh_sa[:, lanes] = one_hot(sea_meta(k, 3).astype(jnp.int32))

    def high(row):
        return jnp.right_shift(row, 7)

    def regrid(field, wide, src_oh, src_cell, dst_oh, dst_cell, weight):
        iota = iota32 if wide else iota8
        total = None
        for k in range(NEAR):
            lanes = slice(k * SL, (k + 1) * SL)
            picked = nn(field(k).astype(BF), src_oh[:, lanes])
            picked = jnp.where(iota == high(src_cell(k)), picked, 0.0)
            if wide:
                value = (picked[0:8] + picked[8:16]) + (picked[16:24] + picked[24:32])
                value = value + pltpu.roll(value, 4, axis=0)
                value = value * weight(k)
                value = jnp.concatenate([value] * 4, axis=0)
            else:
                value = jnp.sum(picked, axis=0, keepdims=True) * weight(k)
            spread = jnp.where(iota == high(dst_cell(k)), value, 0.0).astype(BF)
            part = nt(spread, dst_oh[:, lanes])
            total = part if total is None else total + part
        return total

    def a_air(k):
        return r.air_cells[k]

    def a_sea(k):
        return air_meta(k, 0).astype(jnp.int32)

    def s_sea(k):
        return r.sea_cells[k]

    def s_air(k):
        return sea_meta(k, 3).astype(jnp.int32)

    def field_of(own, arrived, step, by_air):
        def get(k):
            off = k - 2 if by_air else 2 - k
            if off == 0:
                return own[step]
            return arrived[step, OFFS.index(off)]

        return get

    def weights(m):
        g = lambda s: getattr(r, m.name + "_" + s)
        return g

    def stack_taps(m, step, rows, channels):
        g = weights(m)
        w, kc = m.width, m.chans
        lo, hi = channels
        for row in rows:
            lanes = slice(row * w, (row + 1) * w)
            x = g("x")[lo:hi, lanes]
            g("s3")[step, lo:hi, lanes] = roll(x, 1).astype(BF)
            g("s3")[step, kc + lo : kc + hi, lanes] = x.astype(BF)
            g("s3")[step, 2 * kc + lo : 2 * kc + hi, lanes] = roll(x, -1).astype(BF)

    def forward(m, step):
        g = weights(m)
        w, rows = m.width, m.rows
        enc = g("enc")[...]
        for row in range(rows + 4):
            lanes = slice(row * w, (row + 1) * w)
            g("y")[:, lanes] = nn(enc, g("s3")[step, :, lanes])
        fp, y = g("fp"), g("y")
        for q in list(range(rows + 2)):
            feat = y[0:64, q * w : (q + 1) * w]
            feat = feat + y[64:128, (q + 1) * w : (q + 2) * w]
            feat = feat + y[128:192, (q + 2) * w : (q + 3) * w]
            feat = feat.astype(BF).astype(F32)
            if q == 0:
                feat = feat * low_on
            if q == rows + 1:
                feat = feat * up_on
                if m is SEA:
                    below = fp[step, :, rows * w : (rows + 1) * w].astype(BF)
                    feat = feat + last_f * nn(below, r.fold[...])
            fp[step, :, q * w : (q + 1) * w] = feat
        dw = g("dw")[...]
        for row in range(rows):
            mixed = []
            for j in range(3):
                part = None
                for i in range(3):
                    term = dw[:, 3 * i + j : 3 * i + j + 1] * fp[step, :, (row + i) * w : (row + i + 1) * w]
                    part = term if part is None else part + term
                mixed.append(part)
            g("mix")[:, row * w : (row + 1) * w] = mixed[1] + roll(mixed[0], 1) + roll(mixed[2], -1)
        expand, contract, decoder = g("exp")[...], g("con")[...], g("dec")[...]

        def chunk(c, carry):
            lanes = pl.ds(pl.multiple_of(c * 256, 256), 256)
            own = pl.ds(pl.multiple_of(c * 256 + w, 128), 256)
            x = g("mix")[:, lanes]
            x = x - jnp.mean(x, axis=0, keepdims=True)
            rstd = lax.rsqrt(jnp.mean(x * x, axis=0, keepdims=True) + 1e-06)
            x = x * rstd
            g("nrm")[step, :, lanes] = x
            g("rstd")[step, :, lanes] = rstd
            v = nn(expand, x.astype(BF))
            u = v * v
            t = jnp.tanh(v * (C0 + (C0 * C1) * u))
            half = 0.5 + 0.5 * t
            g("dgelu")[step, :, lanes] = half + (0.5 * v) * (1.0 - t * t) * (C0 + (3.0 * C0 * C1) * u)
            hid = (v * half).astype(BF)
            g("hid")[step, :, lanes] = hid
            res = (fp[step, :, own] + nn(contract, hid)).astype(BF)
            g("resb")[step, :, lanes] = res
            g("out")[:, lanes] = nn(decoder, res)
            return carry

        lax.fori_loop(0, SL // 256, chunk, 0)

    def backward(m, step):
        g = weights(m)
        w, rows = m.width, m.rows
        decoder_t, contract_t, expand_t = g("dect")[...], g("cont")[...], g("expt")[...]

        def chunk(c, carry):
            lanes = pl.ds(pl.multiple_of(c * 256, 256), 256)
            dy = g("cot")[:, lanes]
            if m is SEA:
                dy = dy * r.wetf[:, lanes]
            dy = dy.astype(BF)
            g("dyb")[:, lanes] = dy
            dres = nn(decoder_t, dy).astype(BF)
            g("dresb")[:, lanes] = dres
            dhid = nn(contract_t, dres)
            dpre = (dhid * g("dgelu")[step, :, lanes]).astype(BF)
            g("dpreb")[:, lanes] = dpre
            dn = nn(expand_t, dpre)
            x = g("nrm")[step, :, lanes]
            dmean = jnp.mean(dn, axis=0, keepdims=True)
            dproj = jnp.mean(dn * x, axis=0, keepdims=True)
            g("dmr")[1, :, lanes] = g("rstd")[step, :, lanes] * (dn - dmean - x * dproj)
            return carry

        lax.fori_loop(0, SL // 256, chunk, 0)
        fp, dmr = g("fp"), g("dmr")
        dw = g("dw")[...]
        for row in range(rows):
            lanes = slice(row * w, (row + 1) * w)
            d = dmr[1, :, lanes]
            dmr[0, :, lanes] = roll(d, -1)
            dmr[2, :, lanes] = roll(d, 1)
        spare = None
        for q in range(rows + 1, -1, -1):
            total = None
            for i in range(3):
                row = q - i
                if 0 <= row < rows:
                    for j in range(3):
                        term = dw[:, 3 * i + j : 3 * i + j + 1] * dmr[j, :, row * w : (row + 1) * w]
                        total = term if total is None else total + term
            if 1 <= q <= rows:
                total = total + g("dresb")[:, (q - 1) * w : q * w].astype(F32)
            if q == rows + 1:
                if m is SEA:
                    spare = last_f * nt(total.astype(BF), r.fold[...])
                total = total * up_on
            if q == rows and m is SEA:
                total = total + spare
            if q == 0:
                total = total * low_on
            total = total.astype(BF)
            for i in range(3):
                g("dfs")[i * 64 : (i + 1) * 64, (q + i) * w : (q + i + 1) * w] = total
        enc_t = g("enct")[...]
        kc = m.chans
        for row in range(rows + 4):
            lanes = slice(row * w, (row + 1) * w)
            d = nn(enc_t, g("dfs")[:, lanes])
            g("dx")[:, lanes] = d[kc : 2 * kc] + roll(d[0:kc], -1) + roll(d[2 * kc : 3 * kc], 1)

    def weight_grads(m, step):
        g = weights(m)
        w, rows = m.width, m.rows
        row0 = 0 if m is SEA else 64
        fp, dmr = g("fp"), g("dmr")
        exp = nt(g("nrm")[step].astype(BF), g("dpreb")[...])
        for half in range(2):
            start = G_EXP + 2 * row0 + half * 64
            r.g32[start : start + 64, :] += exp[:, half * 128 : (half + 1) * 128]
        con = nt(g("dresb")[...], g("hid")[step])
        for half in range(2):
            start = G_CON + 2 * row0 + half * 64
            r.g32[start : start + 64, :] += con[:, half * 128 : (half + 1) * 128]
        dec = nt(g("dyb")[...], g("resb")[step])
        start = G_DEC + (0 if m is SEA else 48)
        r.g32[start : start + m.outs, 0:64] += dec
        enc = nt(g("dfs")[...], g("s3")[step])
        if m is SEA:
            r.g32[G_ENC0 : G_ENC0 + 192, :] += enc[:, 0:128]
            r.g32[G_ENC1 : G_ENC1 + 192, 0:64] += enc[:, 128:192]
        else:
            r.g32[G_ENC1 : G_ENC1 + 192, 64 : 64 + 48] += enc
        for i in range(3):
            for j in range(3):
                total = None
                for row in range(rows):
                    term = dmr[j, :, row * w : (row + 1) * w] * fp[step, :, (row + i) * w : (row + i + 1) * w]
                    total = term if total is None else total + term
                t = 3 * i + j + (0 if m is SEA else 16)
                r.g32[G_DW : G_DW + 64, t : t + 1] += jnp.sum(total, axis=1, keepdims=True)

    def regrid_flux(step, sent):
        wait(sent)
        flow = regrid(
            field_of(r.pay_f, r.in_f, step, False), True,
            r.oh_sa, s_air, r.oh_ss, s_sea, lambda k: own_weight(k, 2),
        )
        r.pay_g[step] = flow
        sent = [
            send(r.pay_g.at[step], r.in_g.at[step, i], near(off)) for i, off in enumerate((-1, 1))
        ]
        for hi in range(8):
            r.sea_x[48:52, SL + hi * 128 : SL + (hi + 1) * 128] = r.pay_g[step, hi * 4 : hi * 4 + 4, :]
        return sent

    def regrid_surface(step, sent):
        wait(sent)
        skin = regrid(
            field_of(r.pay_s, r.in_s, step, True), False,
            r.oh_as, a_sea, r.oh_aa, a_air, lambda k: air_meta(k, 1),
        )
        r.pay_k[step] = skin
        sent = [
            send(r.pay_k.at[step], r.in_k.at[step, i], near(off)) for i, off in enumerate((-1, 1))
        ]
        for hi in range(8):
            r.air_x[8:9, 256 + hi * 128 : 256 + (hi + 1) * 128] = r.pay_k[step, hi : hi + 1, :]
        return sent

    def sea_states(step, sent):
        r.sea_x[0:48, SL : 2 * SL] = r.halo_s[step].astype(F32)
        wait(sent)
        r.sea_x[0:48, 0:SL] = r.halo_s_in[step, 1].astype(F32) * low_on
        r.sea_x[0:48, 2 * SL : 3 * SL] = r.halo_s_in[step, 0].astype(F32) * up_on
        folded = nn(r.halo_s[step, :, 512:SL], r.fold[...])
        r.sea_x[0:48, 2 * SL : 2 * SL + 512] += last_f * folded
        stack_taps(SEA, step, range(6), (0, 48))

    def sea_forward(step, sent):
        wait(sent)
        for hi in range(8):
            r.sea_x[48:52, hi * 128 : (hi + 1) * 128] = r.in_g[step, 1, hi * 4 : hi * 4 + 4, :] * low_on
            r.sea_x[48:52, 2 * SL + hi * 128 : 2 * SL + (hi + 1) * 128] = (
                r.in_g[step, 0, hi * 4 : hi * 4 + 4, :] * up_on
            )
        folded = nn(r.sea_x[48:64, SL + 512 : 2 * SL].astype(BF), r.fold[...])
        r.sea_x[48:64, 2 * SL : 2 * SL + 512] += last_f * folded
        stack_taps(SEA, step, range(6), (48, 64))
        forward(SEA, step)
        r.o_now[...] += r.wetf[...] * r.sea_out[...]

    def air_states(step, sent):
        r.air_x[0:8, 256 : 256 + SL] = r.a_now[...]
        wait(sent)
        r.air_x[0:8, 0:256] = r.halo_a_in[step, 1] * low_on
        r.air_x[0:8, 256 + SL : 512 + SL] = r.halo_a_in[step, 0] * up_on

    def air_forward(step, sent):
        wait(sent)
        for i in range(2):
            r.air_x[8:9, i * 128 : (i + 1) * 128] = r.in_k[step, 1, 6 + i : 7 + i, :] * low_on
            r.air_x[8:9, 256 + SL + i * 128 : 256 + SL + (i + 1) * 128] = (
                r.in_k[step, 0, i : i + 1, :] * up_on
            )
        stack_taps(AIR, step, range(12), (0, 16))
        forward(AIR, step)
        r.a_now[...] += r.air_out[0:8, :]

    def start_c_sea(step):
        copies = []
        for i, off in enumerate((-1, 1)):
            lanes = slice(i * 2 * SL, i * 2 * SL + SL)
            r.ret_g[step, i] = r.sea_dx[48:56, lanes]
            copies.append(send(r.ret_g.at[step, i], r.ret_g_in.at[step, i], near(off)))
        for i, off in enumerate((-1, 1)):
            lanes = slice(i * 2 * SL, i * 2 * SL + SL)
            r.ret_s[step, i] = r.sea_dx[0:48, lanes].astype(BF)
            copies.append(send(r.ret_s.at[step, i], r.ret_s_in.at[step, i], near(off)))
        back = nt(r.sea_dx[:, 2 * SL : 2 * SL + 512].astype(BF), r.fold[...])
        r.sea_dx[:, SL + 512 : 2 * SL] += last_f * back
        return copies

    def start_c_air(step):
        copies = []
        for i, off in enumerate((-1, 1)):
            start = i * (256 + SL)
            r.ret_a[step, i] = r.air_dx[:, start : start + 256]
            copies.append(send(r.ret_a.at[step, i], r.ret_a_in.at[step, i], near(off)))
        return copies

    def start_dg(step, sent):
        wait(sent[0:2])
        own = slice(SL, 2 * SL)
        r.sea_dx[48:56, own] += r.ret_g_in[step, 1] * low_on + r.ret_g_in[step, 0] * up_on
        for hi in range(8):
            r.pay_dg[step, hi * 4 : hi * 4 + 4, :] = r.sea_dx[48:52, SL + hi * 128 : SL + (hi + 1) * 128]
        return [send(r.pay_dg.at[step], r.in_dg.at[step, i], near(off)) for i, off in enumerate(OFFS)]

    def start_dk(step, sent):
        wait(sent)
        own = slice(256, 512)
        r.air_dx[:, own] += r.ret_a_in[step, 1] * low_on
        own = slice(SL, SL + 256)
        r.air_dx[:, own] += r.ret_a_in[step, 0] * up_on
        for hi in range(8):
            r.pay_dk[step, hi : hi + 1, :] = r.air_dx[8:9, 256 + hi * 128 : 256 + (hi + 1) * 128]
        sent = [send(r.pay_dk.at[step], r.in_dk.at[step, i], near(off)) for i, off in enumerate(OFFS)]
        r.air_cot[0:8, :] += r.air_dx[0:8, 256 : 256 + SL]
        return sent

    def finish_sea_cot(step, sent):
        wait(sent[2:4])
        r.sea_cot[...] += (
            r.sea_dx[0:48, SL : 2 * SL]
            + r.ret_s_in[step, 1].astype(F32) * low_on
            + r.ret_s_in[step, 0].astype(F32) * up_on
        )

    def finish_dg(step, sent):
        wait(sent)
        r.tmp32[...] = regrid(
            field_of(r.pay_dg, r.in_dg, step, True), True,
            r.oh_as, a_sea, r.oh_aa, a_air, lambda k: air_meta(k, 2),
        )
        for hi in range(8):
            r.air_cot[8:12, hi * 128 : (hi + 1) * 128] = r.tmp32[hi * 4 : hi * 4 + 4, :]

    def finish_dk(step, sent):
        wait(sent)
        r.tmp8[...] = regrid(
            field_of(r.pay_dk, r.in_dk, step, False), False,
            r.oh_sa, s_air, r.oh_ss, s_sea, lambda k: own_weight(k, 1),
        )
        for hi in range(8):
            r.sea_cot[0:1, hi * 128 : (hi + 1) * 128] += r.tmp8[hi : hi + 1, :]

    sent_k = regrid_surface(0, sent_s)
    sent_g = regrid_flux(0, sent_f)
    air_states(0, halo_air)
    sea_states(0, halo_sea)
    air_forward(0, sent_k)
    for hi in range(8):
        r.pay_f[1, hi * 4 : hi * 4 + 4, :] = r.air_out[8:12, hi * 128 : (hi + 1) * 128]
    sent_f = start_f(1)
    halo_air = start_halo_air(1)
    sea_forward(0, sent_g)
    sent_s = start_s(1)
    halo_sea = start_halo_sea(1)

    air_states(1, halo_air)
    sent_g = regrid_flux(1, sent_f)
    sea_states(1, halo_sea)
    sent_k = regrid_surface(1, sent_s)
    sea_forward(1, sent_g)
    backward(SEA, 1)
    sea_c = start_c_sea(1)
    for row in range(2):
        r.o_sea[:, row, :] = r.o_now[:, row * 512 : (row + 1) * 512]
    air_forward(1, sent_k)
    backward(AIR, 1)
    air_c = start_c_air(1)
    for row in range(8):
        r.o_air[:, row, :] = r.a_now[:, row * 128 : (row + 1) * 128]

    weight_grads(SEA, 1)
    sent_dg = start_dg(1, sea_c)
    weight_grads(AIR, 1)
    finish_sea_cot(1, sea_c)
    sent_dk = start_dk(1, air_c)
    finish_dg(1, sent_dg)
    backward(AIR, 0)
    air_c = start_c_air(0)
    weight_grads(AIR, 0)
    finish_dk(1, sent_dk)
    backward(SEA, 0)
    sea_c = start_c_sea(0)
    weight_grads(SEA, 0)

    for c in range(2):
        for y in range(4):
            for e in range(8):
                start = ((c * 4 + y) * 8 + e) * 16
                r.gb[c, y, e] = r.g32[start : start + 16, :].astype(BF)
    sum_core = [send(r.gb.at[1 - core], r.r1, peer_core)]
    sent_dk = start_dk(0, air_c)
    wait(sum_core)
    r.h1[...] = (r.gb[core].astype(F32) + r.r1[...].astype(F32)).astype(BF)
    sum_y = [
        send(r.h1.at[lax.rem(yy + s, 4)], r.r2.at[s - 1], peers_y[s - 1]) for s in (1, 2, 3)
    ]
    for row in range(8):
        r.o_dair[:, row, :] = r.air_cot[0:8, row * 128 : (row + 1) * 128]
    sent_dg = start_dg(0, sea_c)
    wait(sum_y)
    h2 = r.h1[yy].astype(F32)
    for s in range(3):
        h2 = h2 + r.r2[s].astype(F32)
    h2 = h2.astype(BF)
    r.h2[...] = h2
    r.r3[xx] = h2
    sum_x = [send(r.h2, r.r3.at[xx], dev) for dev in peers_x]
    finish_sea_cot(0, sea_c)
    finish_dk(0, sent_dk)
    for row in range(2):
        r.o_dsea[:, row, :] = r.sea_cot[:, row * 512 : (row + 1) * 512]
    wait(sum_x)
    h3 = r.r3[0].astype(F32)
    for s in range(1, nx):
        h3 = h3 + r.r3[s].astype(F32)
    h3 = h3.astype(BF)
    r.h3[...] = h3
    r.r4[zz] = h3
    sum_z = [send(r.h3, r.r4.at[zz], dev) for dev in peers_z]
    finish_dg(0, sent_dg)
    for row in range(8):
        r.o_dflux[:, row, :] = r.air_cot[8:12, row * 128 : (row + 1) * 128]
    wait(sum_z)
    h4 = r.r4[0].astype(F32)
    for s in range(1, nz):
        h4 = h4 + r.r4[s].astype(F32)
    r.gout[core, yy] = h4.astype(BF)
    give_y = [send(r.gout.at[core, yy], r.gout.at[core, yy], dev) for dev in peers_y]
    wait(give_y)
    give_core = [send(r.gout.at[core], r.gout.at[core], peer_core)]
    wait(give_core)
    r.o_grads[...] = r.gout[...]


def finish(n, *refs):
    given, results = refs[0:5], refs[6:11]
    r = Names(
        ("grads",) + tuple("o_" + m + "_" + w for m in ("air", "sea") for w in WEIGHTS) + ("g32",),
        (refs[5],) + refs[11:],
    )
    for a, b in zip(given, results):
        b[...] = a[...]
    for c in range(2):
        for y in range(4):
            for e in range(8):
                start = ((c * 4 + y) * 8 + e) * 16
                r.g32[start : start + 16, :] = r.grads[c, y, e].astype(F32)

    scale = 1.0 / math.sqrt(SL * n)
    for m in (AIR, SEA):
        o = lambda s: getattr(r, "o_" + m.name + "_" + s)
        col = 0 if m is SEA else 64
        for half in range(2):
            start = G_EXP + 2 * col + half * 64
            o("exp")[:, half * 128 : (half + 1) * 128] = r.g32[start : start + 64, :] * scale
            start = G_CON + 2 * col + half * 64
            o("con")[:, half * 128 : (half + 1) * 128] = r.g32[start : start + 64, :] * scale
        start = G_DEC + (0 if m is SEA else 48)
        count_out = 48 if m is SEA else 12
        o("dec")[...] = r.g32[start : start + count_out, 0:64] * scale
        shift = 0 if m is SEA else 16
        o("dw")[...] = (jnp.transpose(r.g32[G_DW : G_DW + 64, :]) * scale)[shift : shift + 9, :]
        chans = 52 if m is SEA else 9
        for i in range(3):
            for j in range(3):
                t = 3 * i + j
                if m is AIR:
                    base, left = G_ENC1, 64 + 16 * j
                else:
                    base, left = (G_ENC0, 64 * j) if j < 2 else (G_ENC1, 0)
                piece = r.g32[base + i * 64 : base + (i + 1) * 64, left : left + chans]
                o("enc")[:, t * chans : (t + 1) * chans] = piece * scale


def body(n, *args):
    (
        air_state, sea_state, flux, air_cells, sea_cells, counts, sea_share, air_share, partner, wet,
        air_c, sea_c, air_enc, air_dw, air_exp, air_con, air_dec, sea_enc, sea_dw, sea_exp, sea_con,
        sea_dec,
    ) = args
    slots = lambda x: jnp.transpose(x, (1, 0, 2))
    given = [
        air_state, sea_state, flux, slots(air_cells), slots(sea_cells), counts, slots(sea_share),
        slots(air_share), partner[None], wet, air_c, sea_c,
        air_enc, air_dw.T, air_exp.T, air_con, air_dec, sea_enc, sea_dw.T, sea_exp.T, sea_con, sea_dec,
    ]
    vmem = pl.BlockSpec(memory_space=pltpu.VMEM)
    fields = [jax.ShapeDtypeStruct(x.shape, F32) for x in (air_state, sea_state, air_c, sea_c, flux)]
    made = pl.pallas_call(
        lambda *refs: kernel(n, *refs),
        out_shape=fields + [jax.ShapeDtypeStruct((2, 4, 8, 16, 128), BF)],
        in_specs=[vmem] * len(given),
        out_specs=[vmem] * 6,
        scratch_shapes=[pltpu.VMEM(shape, kind) for _, shape, kind in scratch_list()]
        + [pltpu.SemaphoreType.DMA((COPIES,)), pltpu.SemaphoreType.DMA((COPIES,))],
        compiler_params=pltpu.CompilerParams(
            collective_id=0, has_side_effects=True, vmem_limit_bytes=60 * 1024 * 1024
        ),
        name="coupled",
    )(*given)
    grads = [air_enc, air_dw.T, air_exp.T, air_con, air_dec, sea_enc, sea_dw.T, sea_exp.T, sea_con, sea_dec]
    done = pl.pallas_call(
        lambda *refs: finish(n, *refs),
        out_shape=fields + [jax.ShapeDtypeStruct(x.shape, F32) for x in grads],
        in_specs=[vmem] * 6,
        out_specs=[vmem] * 15,
        scratch_shapes=[pltpu.VMEM((GROWS, 128), F32)],
        name="finish",
    )(*made)
    done = list(done)
    for i in (6, 7, 11, 12):
        done[i] = done[i].T
    return done


def solution(mesh):
    n = mesh.shape["tile"]
    rows = P(None, "tile", None)
    slots = P("tile", None, None)
    return jax.shard_map(
        lambda *args: tuple(body(n, *args)),
        mesh=mesh,
        in_specs=(rows, rows, rows, slots, slots, P("tile", None), slots, slots, P(), P("tile", None), rows, rows)
        + (P(),) * 10,
        out_specs=(rows,) * 5 + (P(),) * 10,
        check_vma=False,
    )
```

time: 1040 us -> 88.6 us (0.09)
  the two profiles are of different devices: /device:TPU:33 before, /device:TPU:1 now
where the time goes in v1:
time: 88.6 us; the launch traced here: 88.5 us
  Pallas kernels  87.7 us (99%)
    pallas_call x1, Pallas kernels, body(): pl.pallas_call(lambda *refs: kernel(n, *refs), out_shape=fields + [jax.Sh...  85.4 us
    pallas_call x1, Pallas kernels, body(): pl.pallas_call(lambda *refs: finish(n, *refs), out_shape=fields + [jax.Sh...  2.3 us

profile of v1, /device:TPU:1, one launch (start us, length us, event | category | flops | bytes accessed | tf_op | source)
XLA Modules:
  0.0 88.5 jit_solution(12638127784157858198)
XLA Ops:
  0.7 85.4 %coupled.1 = (f32[8,8,128]{2,1,0:T(8,128)}, f32[48,2,512]{2,1,0:T(2,128)}, f32[8,8,128]{2,1,0:T(8,128)}, f32[48,2,512]{2,1,0:T(2,128)}, f32[4,8,128]{2,1,0:T(8,128)}, /*index=5*/bf16[2,4,8,16,128]{4,3,2,1,0:T(8,128)(2,1)}) custom-call(f32[8,8,128]{2,1,0:T(8,128)} %refs_0_.1, f32[48,2,512]{2,1,0:T(2,128)} %refs_1_.1, f32[4,8,128]{2,1,0:T(8,128)} %refs_2_.1, ...), custom_call_target="tpu_custom_call" | custom-call | tf_op jit(solution)/shard_map/coupled/pallas_call | solution.py:826
  86.0 2.3 %finish.1 = (f32[8,8,128]{2,1,0:T(8,128)}, f32[48,2,512]{2,1,0:T(2,128)}, f32[8,8,128]{2,1,0:T(8,128)}, f32[48,2,512]{2,1,0:T(2,128)}, f32[4,8,128]{2,1,0:T(8,12...) custom-call(f32[8,8,128]{2,1,0:T(8,128)} %get-tuple-element.36.refs_, ...), custom_call_target="tpu_custom_call" | custom-call | tf_op jit(solution)/shard_map/finish/pallas_call | solution.py:839

commit v2 on v1

--- a/solution.py
+++ b/solution.py
@@ -11,6 +11,7 @@
 F32 = jnp.float32
 BF = jnp.bfloat16
 OFFS = (-2, -1, 1, 2)
+AROUND = (-2, -1, 0, 1, 2)
 NEAR = 5
 SL = 1024
 C0 = math.sqrt(2.0 / math.pi)
@@ -31,6 +32,23 @@
 
 def roll(x, by):
     return pltpu.roll(x, by % x.shape[1], axis=1)
+
+
+def at_band(z, xr, y, core, nx, flip):
+    return ((z * nx + xr) * 4 + flip(y, 4, lax.rem(xr, 2))) * 2 + core
+
+
+class Either:
+    def __init__(self, own, local, remote):
+        self.own, self.local, self.remote = own, local, remote
+
+    def start(self):
+        pl.when(self.own)(self.local.start)
+        pl.when(jnp.logical_not(self.own))(self.remote.start)
+
+    def wait(self):
+        pl.when(self.own)(self.local.wait)
+        pl.when(jnp.logical_not(self.own))(self.remote.wait)
 
 
 class Names:
@@ -112,7 +130,7 @@
 OUTPUTS = ("o_air", "o_sea", "o_dair", "o_dsea", "o_dflux", "o_grads")
 WEIGHTS = ("enc", "dw", "exp", "con", "dec")
 
-COPIES = 80
+COPIES = 96
 GROWS = 1024
 G_EXP, G_CON, G_ENC0, G_ENC1, G_DEC, G_DW = 0, 256, 512, 704, 896, 960
 
@@ -121,8 +139,24 @@
     f, b = F32, BF
     items = AIR.scratch() + SEA.scratch()
     items += [
-        ("meta_pay", (4, 8, SL), f),
-        ("meta_in", (NEAR, 8, SL), f),
+        ("meta_pay", (4, 4, SL), f),
+        ("meta_in", (4, 4, SL), f),
+        ("own_f", (32, SL), f),
+        ("own_pay", (32, SL), b),
+        ("own_in", (32, SL), b),
+        ("own", (24, SL), f),
+        ("band_a", (8, SL), f),
+        ("band_a_in", (8, SL), f),
+        ("cots", (48, SL), b),
+        ("cots_in", (48, SL), b),
+        ("cota", (8, SL), f),
+        ("cota_in", (8, SL), f),
+        ("home_air", (8, SL), f),
+        ("home_sea", (48, SL), b),
+        ("back_sea", (48, SL), b),
+        ("home_dair", (16, SL), f),
+        ("home_dsea", (48, SL), b),
+        ("back_dsea", (48, SL), b),
         ("oh_aa", (128, NEAR * SL), b),
         ("oh_as", (128, NEAR * SL), b),
         ("oh_sa", (128, NEAR * SL), b),
@@ -131,12 +165,13 @@
         ("wetf", (1, SL), f),
         ("a_now", (8, SL), f),
         ("o_now", (48, SL), f),
-        ("pay_f", (2, 32, 128), f),
-        ("in_f", (2, 4, 32, 128), f),
+        ("new_f", (32, 128), f),
+        ("pay_f", (2, 32, 128), b),
+        ("in_f", (2, 5, 32, 128), b),
         ("pay_s", (2, 8, 128), f),
-        ("in_s", (2, 4, 8, 128), f),
+        ("in_s", (2, 5, 8, 128), f),
         ("halo_s", (2, 48, SL), b),
-        ("halo_s_in", (2, 2, 48, SL), b),
+        ("halo_s_in", (2, 3, 48, SL), b),
         ("halo_a", (2, 2, 8, 256), f),
         ("halo_a_in", (2, 2, 8, 256), f),
         ("pay_g", (2, 32, 128), f),
@@ -179,14 +214,29 @@
     nz = n // (8 * nx)
     xx = lax.rem(me // 8, nx)
     zz = me // (8 * nx)
-    first = me == 0
-    last = me == n - 1
+
+    def flip(value, size, odd):
+        return value + odd * (size - 1 - 2 * value)
+
+    def worker(band):
+        c, chip = lax.rem(band, 2), band // 2
+        z, xr, yr = chip // (4 * nx), lax.rem(chip // 4, nx), lax.rem(chip, 4)
+        x = flip(xr, nx, lax.rem(z, 2))
+        y = flip(yr, 4, lax.rem(xr, 2))
+        return ((z * nx + x) * 4 + y) * 2 + c
+
+    band = at_band(zz, flip(xx, nx, lax.rem(zz, 2)), yy, core, nx, flip)
+    first = band == 0
+    last = band == n - 1
     low_on = jnp.where(first, 0.0, 1.0).astype(F32)
     up_on = jnp.where(last, 0.0, 1.0).astype(F32)
     last_f = 1.0 - up_on
 
     def near(off):
-        return lax.rem(me + (off + n), n)
+        return worker(lax.rem(band + (off + n), n))
+
+    def served(off):
+        return worker(lax.rem(me + (off + n), n))
 
     def at(z, x, y, c):
         return ((z * nx + x) * 4 + y) * 2 + c
@@ -197,6 +247,21 @@
     peers_z = [at(lax.rem(zz + s, nz), xx, yy, core) for s in range(1, nz)]
 
     count = [0]
+
+    def give(src, dst, dev):
+        i = count[0]
+        count[0] += 1
+        remote = pltpu.make_async_remote_copy(
+            src_ref=src,
+            dst_ref=dst,
+            send_sem=r.ssem.at[i],
+            recv_sem=r.rsem.at[i],
+            device_id=(dev,),
+            device_id_type=MESH,
+        )
+        copy = Either(dev == me, pltpu.make_async_copy(src, dst, r.rsem.at[i]), remote)
+        copy.start()
+        return copy
 
     def send(src, dst, dev):
         i = count[0]
@@ -219,49 +284,82 @@
     iota8 = lax.broadcasted_iota(jnp.int32, (8, SL), 0)
     iota32 = lax.broadcasted_iota(jnp.int32, (32, SL), 0) // 4
 
-    everyone = [near(off) for off in OFFS] + peers_y + peers_x + peers_z
+    senders = [near(off) for off in OFFS] + peers_y + peers_x + peers_z
     barrier = pltpu.get_barrier_semaphore()
-    for dev in everyone:
+    for dev in senders:
         pl.semaphore_signal(barrier, inc=1, device_id=(dev,), device_id_type=MESH)
+    either = [lax.rem(band + (n - off), n) for off in AROUND] + [worker(me)]
+
+    def greet(dev):
+        def there():
+            pl.semaphore_signal(barrier, inc=1, device_id=(dev,), device_id_type=MESH)
+
+        pl.when(dev != me)(there)
+
+    greetings = len(senders)
+    for dev in either:
+        greet(dev)
+        greetings = greetings + (dev != me).astype(jnp.int32)
 
     lane = lax.broadcasted_iota(jnp.int32, (1, SL), 1)
 
-    def meta_rows(k_out, k_air, ref, i):
+    def slot_rows(k_out, k_air, put):
         used = lane < r.counts[0:1, k_out : k_out + 1]
-        ref[i, 0:1, :] = r.sea_cells[k_out].astype(F32)
-        ref[i, 1:2, :] = jnp.where(used, r.air_share[k_out], 0.0)
-        ref[i, 2:3, :] = jnp.where(used, r.sea_share[k_out], 0.0)
-        ref[i, 3:4, :] = r.air_cells[k_air].astype(F32)
-
-    r.meta_pay[...] = jnp.zeros_like(r.meta_pay)
+        put(0, r.sea_cells[k_out].astype(F32))
+        put(1, jnp.where(used, r.air_share[k_out], 0.0))
+        put(2, jnp.where(used, r.sea_share[k_out], 0.0))
+        put(3, r.air_cells[k_air].astype(F32))
+
     for i, off in enumerate(OFFS):
-        meta_rows(off + 2, 2 - off, r.meta_pay, i)
-
+
+        def put(row, value, i=i):
+            r.meta_pay[i, row : row + 1, :] = value
+
+        slot_rows(off + 2, 2 - off, put)
+    for k in range(NEAR):
+
+        def put(row, value, k=k):
+            base = 6 * k
+            if row in (1, 2):
+                r.own_f[base + 3 + row : base + 4 + row, :] = value
+            else:
+                high = jnp.floor(value * (1.0 / 128.0))
+                start = base + (0 if row == 0 else 2)
+                r.own_f[start : start + 1, :] = high
+                r.own_f[start + 1 : start + 2, :] = value - 128.0 * high
+
+        slot_rows(k, k, put)
+    r.own_f[31:32, :] = jnp.zeros((1, SL), F32)
     for row in range(8):
         lanes = slice(row * 128, (row + 1) * 128)
-        r.a_now[:, lanes] = r.air_state[:, row, :]
-        r.air_cot[0:8, lanes] = r.air_c[:, row, :]
-        r.pay_f[0, row * 4 : row * 4 + 4, :] = r.flux[:, row, :]
-    r.air_cot[8:16, :] = jnp.zeros((8, SL), F32)
+        r.band_a[:, lanes] = r.air_state[:, row, :]
+        r.cota[:, lanes] = r.air_c[:, row, :]
+        r.new_f[row * 4 : row * 4 + 4, :] = r.flux[:, row, :]
     for row in range(2):
         lanes = slice(row * 512, (row + 1) * 512)
-        r.o_now[:, lanes] = r.sea_state[:, row, :]
-        r.sea_cot[:, lanes] = r.sea_c[:, row, :]
-        r.wetf[:, lanes] = r.wet[row : row + 1, :].astype(F32)
+        r.halo_s[0, :, lanes] = r.sea_state[:, row, :].astype(BF)
+        r.own_f[30:31, lanes] = r.wet[row : row + 1, :].astype(F32)
+    for hi in range(8):
+        row, left = hi // 4, (hi % 4) * 128
+        r.pay_s[0, hi : hi + 1, :] = r.sea_state[0, row : row + 1, left : left + 128]
+    r.pay_f[0] = r.new_f[...].astype(BF)
+    r.own_pay[...] = r.own_f[...].astype(BF)
+    r.halo_a[0, 0] = r.band_a[:, 0:256]
+    r.halo_a[0, 1] = r.band_a[:, SL - 256 : SL]
 
     def start_f(step):
-        return [send(r.pay_f.at[step], r.in_f.at[step, i], near(off)) for i, off in enumerate(OFFS)]
+        return [send(r.pay_f.at[step], r.in_f.at[step, off + 2], near(off)) for off in OFFS]
 
     def start_s(step):
         for hi in range(8):
             r.pay_s[step, hi : hi + 1, :] = r.o_now[0:1, hi * 128 : (hi + 1) * 128]
-        return [send(r.pay_s.at[step], r.in_s.at[step, i], near(off)) for i, off in enumerate(OFFS)]
+        return [send(r.pay_s.at[step], r.in_s.at[step, off + 2], near(off)) for off in OFFS]
 
     def start_halo_sea(step):
         r.halo_s[step] = r.o_now[...].astype(BF)
         return [
-            send(r.halo_s.at[step], r.halo_s_in.at[step, i], near(off))
-            for i, off in enumerate((-1, 1))
+            send(r.halo_s.at[step], r.halo_s_in.at[step, off + 1], near(off))
+            for off in (-1, 1)
         ]
 
     def start_halo_air(step):
@@ -272,13 +370,19 @@
             for i, off in enumerate((-1, 1))
         ]
 
-    pl.semaphore_wait(barrier, len(everyone))
-    metas = [
-        send(r.meta_pay.at[i], r.meta_in.at[off + 2], near(off)) for i, off in enumerate(OFFS)
-    ]
-    sent_s, sent_f = start_s(0), start_f(0)
-    halo_air, halo_sea = start_halo_air(0), start_halo_sea(0)
-    meta_rows(2, 2, r.meta_in, 2)
+    pl.semaphore_wait(barrier, greetings)
+    metas = [give(r.own_pay, r.own_in, served(0))]
+    for i, off in enumerate(OFFS):
+        metas.append(give(r.meta_pay.at[i], r.meta_in.at[i], served(off)))
+    sent_s = [give(r.pay_s.at[0], r.in_s.at[0, off + 2], served(off)) for off in AROUND]
+    sent_f = [give(r.pay_f.at[0], r.in_f.at[0, off + 2], served(off)) for off in AROUND]
+    halo_air = [give(r.band_a, r.band_a_in, served(0))]
+    for i, off in enumerate((-1, 1)):
+        halo_air.append(give(r.halo_a.at[0, i], r.halo_a_in.at[0, i], served(off)))
+    own_sea = [give(r.halo_s.at[0], r.halo_s_in.at[0, 1], served(0))]
+    for row in range(2):
+        lanes = slice(row * 512, (row + 1) * 512)
+        r.cots[:, lanes] = r.sea_c[:, row, :].astype(BF)
 
     r.g32[...] = jnp.zeros_like(r.g32)
     for m in (AIR, SEA):
@@ -314,27 +418,46 @@
         low = jnp.bitwise_and(row, 127)
         return jnp.where(iota128 == low, 1.0, 0.0).astype(BF)
 
+    def own_row(k, row):
+        return r.own[4 * k + row : 4 * k + row + 1, :]
+
+    def air_meta(k, row):
+        if k == 2:
+            return own_row(2, row)
+        return r.meta_in[OFFS.index(k - 2), row : row + 1, :]
+
+    def sea_meta(k, row):
+        return air_meta(4 - k, row)
+
+    def own_weight(k, row):
+        return own_row(k, row)
+
+    def a_air(k):
+        return own_row(k, 3).astype(jnp.int32)
+
+    def a_sea(k):
+        return air_meta(k, 0).astype(jnp.int32)
+
+    def s_sea(k):
+        return own_row(k, 0).astype(jnp.int32)
+
+    def s_air(k):
+        return sea_meta(k, 3).astype(jnp.int32)
+
+    wait(metas)
+    arrived = r.own_in[...].astype(F32)
+    for k in range(NEAR):
+        base = 6 * k
+        r.own[4 * k : 4 * k + 1, :] = arrived[base : base + 1] * 128.0 + arrived[base + 1 : base + 2]
+        r.own[4 * k + 1 : 4 * k + 3, :] = arrived[base + 4 : base + 6]
+        r.own[4 * k + 3 : 4 * k + 4, :] = arrived[base + 2 : base + 3] * 128.0 + arrived[base + 3 : base + 4]
+    r.wetf[...] = arrived[30:31]
     for k in range(NEAR):
         lanes = slice(k * SL, (k + 1) * SL)
-        r.oh_aa[:, lanes] = one_hot(r.air_cells[k])
-        r.oh_ss[:, lanes] = one_hot(r.sea_cells[k])
-
-    def air_meta(k, row):
-        return r.meta_in[k, row : row + 1, :]
-
-    def sea_meta(k, row):
-        return r.meta_in[4 - k, row : row + 1, :]
-
-    def own_weight(k, row):
-        share = r.air_share if row == 1 else r.sea_share
-        used = lane < r.counts[0:1, k : k + 1]
-        return jnp.where(used, share[k], 0.0)
-
-    wait(metas)
-    for k in range(NEAR):
-        lanes = slice(k * SL, (k + 1) * SL)
-        r.oh_as[:, lanes] = one_hot(air_meta(k, 0).astype(jnp.int32))
-        r.oh_sa[:, lanes] = one_hot(sea_meta(k, 3).astype(jnp.int32))
+        r.oh_aa[:, lanes] = one_hot(a_air(k))
+        r.oh_ss[:, lanes] = one_hot(s_sea(k))
+        r.oh_as[:, lanes] = one_hot(a_sea(k))
+        r.oh_sa[:, lanes] = one_hot(s_air(k))
 
     def high(row):
         return jnp.right_shift(row, 7)
@@ -358,24 +481,12 @@
             total = part if total is None else total + part
         return total
 
-    def a_air(k):
-        return r.air_cells[k]
-
-    def a_sea(k):
-        return air_meta(k, 0).astype(jnp.int32)
-
-    def s_sea(k):
-        return r.sea_cells[k]
-
-    def s_air(k):
-        return sea_meta(k, 3).astype(jnp.int32)
-
     def field_of(own, arrived, step, by_air):
         def get(k):
             off = k - 2 if by_air else 2 - k
-            if off == 0:
+            if off == 0 and not (arrived.shape[1] == NEAR and step == 0):
                 return own[step]
-            return arrived[step, OFFS.index(off)]
+            return arrived[step, (AROUND if arrived.shape[1] == NEAR else OFFS).index(off)]
 
         return get
 
@@ -571,11 +682,14 @@
         return sent
 
     def sea_states(step, sent):
-        r.sea_x[0:48, SL : 2 * SL] = r.halo_s[step].astype(F32)
         wait(sent)
-        r.sea_x[0:48, 0:SL] = r.halo_s_in[step, 1].astype(F32) * low_on
+        own = r.halo_s[1] if step else r.halo_s_in[0, 1]
+        r.sea_x[0:48, SL : 2 * SL] = own.astype(F32)
+        if step == 0:
+            r.o_now[...] = own.astype(F32)
+        r.sea_x[0:48, 0:SL] = r.halo_s_in[step, 2].astype(F32) * low_on
         r.sea_x[0:48, 2 * SL : 3 * SL] = r.halo_s_in[step, 0].astype(F32) * up_on
-        folded = nn(r.halo_s[step, :, 512:SL], r.fold[...])
+        folded = nn(own[:, 512:SL], r.fold[...])
         r.sea_x[0:48, 2 * SL : 2 * SL + 512] += last_f * folded
         stack_taps(SEA, step, range(6), (0, 48))
 
@@ -593,8 +707,10 @@
         r.o_now[...] += r.wetf[...] * r.sea_out[...]
 
     def air_states(step, sent):
+        wait(sent)
+        if step == 0:
+            r.a_now[...] = r.band_a_in[...]
         r.air_x[0:8, 256 : 256 + SL] = r.a_now[...]
-        wait(sent)
         r.air_x[0:8, 0:256] = r.halo_a_in[step, 1] * low_on
         r.air_x[0:8, 256 + SL : 512 + SL] = r.halo_a_in[step, 0] * up_on
 
@@ -677,13 +793,19 @@
         for hi in range(8):
             r.sea_cot[0:1, hi * 128 : (hi + 1) * 128] += r.tmp8[hi : hi + 1, :]
 
+    wait(own_sea)
+    halo_sea = [
+        send(r.halo_s_in.at[0, 1], r.halo_s_in.at[0, off + 1], near(off)) for off in (-1, 1)
+    ]
     sent_k = regrid_surface(0, sent_s)
     sent_g = regrid_flux(0, sent_f)
+    sent_cot = [give(r.cota, r.cota_in, served(0)), give(r.cots, r.cots_in, served(0))]
     air_states(0, halo_air)
     sea_states(0, halo_sea)
     air_forward(0, sent_k)
     for hi in range(8):
-        r.pay_f[1, hi * 4 : hi * 4 + 4, :] = r.air_out[8:12, hi * 128 : (hi + 1) * 128]
+        r.new_f[hi * 4 : hi * 4 + 4, :] = r.air_out[8:12, hi * 128 : (hi + 1) * 128]
+    r.pay_f[1] = r.new_f[...].astype(BF)
     sent_f = start_f(1)
     halo_air = start_halo_air(1)
     sea_forward(0, sent_g)
@@ -695,21 +817,23 @@
     sea_states(1, halo_sea)
     sent_k = regrid_surface(1, sent_s)
     sea_forward(1, sent_g)
+    wait(sent_cot)
+    r.sea_cot[...] = r.cots_in[...].astype(F32)
+    r.air_cot[0:8, :] = r.cota_in[...]
+    r.air_cot[8:16, :] = jnp.zeros((8, SL), F32)
     backward(SEA, 1)
     sea_c = start_c_sea(1)
-    for row in range(2):
-        r.o_sea[:, row, :] = r.o_now[:, row * 512 : (row + 1) * 512]
     air_forward(1, sent_k)
     backward(AIR, 1)
     air_c = start_c_air(1)
-    for row in range(8):
-        r.o_air[:, row, :] = r.a_now[:, row * 128 : (row + 1) * 128]
 
     weight_grads(SEA, 1)
     sent_dg = start_dg(1, sea_c)
     weight_grads(AIR, 1)
     finish_sea_cot(1, sea_c)
     sent_dk = start_dk(1, air_c)
+    r.back_sea[...] = r.o_now[...].astype(BF)
+    home = [give(r.a_now, r.home_air, band), give(r.back_sea, r.home_sea, band)]
     finish_dg(1, sent_dg)
     backward(AIR, 0)
     air_c = start_c_air(0)
@@ -731,8 +855,11 @@
     sum_y = [
         send(r.h1.at[lax.rem(yy + s, 4)], r.r2.at[s - 1], peers_y[s - 1]) for s in (1, 2, 3)
     ]
+    wait(home)
     for row in range(8):
-        r.o_dair[:, row, :] = r.air_cot[0:8, row * 128 : (row + 1) * 128]
+        r.o_air[:, row, :] = r.home_air[:, row * 128 : (row + 1) * 128]
+    for row in range(2):
+        r.o_sea[:, row, :] = r.home_sea[:, row * 512 : (row + 1) * 512].astype(F32)
     sent_dg = start_dg(0, sea_c)
     wait(sum_y)
     h2 = r.h1[yy].astype(F32)
@@ -744,8 +871,7 @@
     sum_x = [send(r.h2, r.r3.at[xx], dev) for dev in peers_x]
     finish_sea_cot(0, sea_c)
     finish_dk(0, sent_dk)
-    for row in range(2):
-        r.o_dsea[:, row, :] = r.sea_cot[:, row * 512 : (row + 1) * 512]
+    r.back_dsea[...] = r.sea_cot[...].astype(BF)
     wait(sum_x)
     h3 = r.r3[0].astype(F32)
     for s in range(1, nx):
@@ -755,14 +881,20 @@
     r.r4[zz] = h3
     sum_z = [send(r.h3, r.r4.at[zz], dev) for dev in peers_z]
     finish_dg(0, sent_dg)
-    for row in range(8):
-        r.o_dflux[:, row, :] = r.air_cot[8:12, row * 128 : (row + 1) * 128]
+    home = [give(r.air_cot, r.home_dair, band), give(r.back_dsea, r.home_dsea, band)]
     wait(sum_z)
     h4 = r.r4[0].astype(F32)
     for s in range(1, nz):
         h4 = h4 + r.r4[s].astype(F32)
     r.gout[core, yy] = h4.astype(BF)
     give_y = [send(r.gout.at[core, yy], r.gout.at[core, yy], dev) for dev in peers_y]
+    wait(home)
+    for row in range(8):
+        lanes = slice(row * 128, (row + 1) * 128)
+        r.o_dair[:, row, :] = r.home_dair[0:8, lanes]
+        r.o_dflux[:, row, :] = r.home_dair[8:12, lanes]
+    for row in range(2):
+        r.o_dsea[:, row, :] = r.home_dsea[:, row * 512 : (row + 1) * 512].astype(F32)
     wait(give_y)
     give_core = [send(r.gout.at[core], r.gout.at[core], peer_core)]
     wait(give_core)

time: 88.6 us -> 85.4 us (0.964)
  Pallas kernels: 87.7 us -> 84.5 us
    pallas_call x1, Pallas kernels: 85.4 us -> 82.2 us  [body(): pl.pallas_call(lambda *refs: kernel(n, *refs), out_shape=fields + [jax.Sh...]
where the time goes in v2:
time: 85.4 us; the launch traced here: 85.3 us
  Pallas kernels  84.5 us (99%)
    pallas_call x1, Pallas kernels, body(): pl.pallas_call(lambda *refs: kernel(n, *refs), out_shape=fields + [jax.Sh...  82.2 us
    pallas_call x1, Pallas kernels, body(): pl.pallas_call(lambda *refs: finish(n, *refs), out_shape=fields + [jax.Sh...  2.3 us

profile of v2, /device:TPU:1, one launch (start us, length us, event | category | flops | bytes accessed | tf_op | source)
XLA Modules:
  0.0 85.3 jit_solution(4088836888438277449)
XLA Ops:
  0.7 82.2 %coupled.1 = (f32[8,8,128]{2,1,0:T(8,128)}, f32[48,2,512]{2,1,0:T(2,128)}, f32[8,8,128]{2,1,0:T(8,128)}, f32[48,2,512]{2,1,0:T(2,128)}, f32[4,8,128]{2,1,0:T(8,128)}, /*index=5*/bf16[2,4,8,16,128]{4,3,2,1,0:T(8,128)(2,1)}) custom-call(f32[8,8,128]{2,1,0:T(8,128)} %refs_0_.1, f32[48,2,512]{2,1,0:T(2,128)} %refs_1_.1, f32[4,8,128]{2,1,0:T(8,128)} %refs_2_.1, ...), custom_call_target="tpu_custom_call" | custom-call | tf_op jit(solution)/shard_map/coupled/pallas_call | solution.py:958
  82.8 2.3 %finish.1 = (f32[8,8,128]{2,1,0:T(8,128)}, f32[48,2,512]{2,1,0:T(2,128)}, f32[8,8,128]{2,1,0:T(8,128)}, f32[48,2,512]{2,1,0:T(2,128)}, f32[4,8,128]{2,1,0:T(8,12...) custom-call(f32[8,8,128]{2,1,0:T(8,128)} %get-tuple-element.36.refs_, ...), custom_call_target="tpu_custom_call" | custom-call | tf_op jit(solution)/shard_map/finish/pallas_call | solution.py:971

commit v3 on v2

--- a/solution.py
+++ b/solution.py
@@ -14,6 +14,7 @@
 AROUND = (-2, -1, 0, 1, 2)
 NEAR = 5
 SL = 1024
+PART = 1024
 C0 = math.sqrt(2.0 / math.pi)
 C1 = 0.044715
 
@@ -538,9 +539,9 @@
             g("mix")[:, row * w : (row + 1) * w] = mixed[1] + roll(mixed[0], 1) + roll(mixed[2], -1)
         expand, contract, decoder = g("exp")[...], g("con")[...], g("dec")[...]
 
-        def chunk(c, carry):
-            lanes = pl.ds(pl.multiple_of(c * 256, 256), 256)
-            own = pl.ds(pl.multiple_of(c * 256 + w, 128), 256)
+        def chunk(c):
+            lanes = slice(c * PART, (c + 1) * PART)
+            own = slice(c * PART + w, (c + 1) * PART + w)
             x = g("mix")[:, lanes]
             x = x - jnp.mean(x, axis=0, keepdims=True)
             rstd = lax.rsqrt(jnp.mean(x * x, axis=0, keepdims=True) + 1e-06)
@@ -557,17 +558,17 @@
             res = (fp[step, :, own] + nn(contract, hid)).astype(BF)
             g("resb")[step, :, lanes] = res
             g("out")[:, lanes] = nn(decoder, res)
-            return carry
-
-        lax.fori_loop(0, SL // 256, chunk, 0)
+
+        for c in range(SL // PART):
+            chunk(c)
 
     def backward(m, step):
         g = weights(m)
         w, rows = m.width, m.rows
         decoder_t, contract_t, expand_t = g("dect")[...], g("cont")[...], g("expt")[...]
 
-        def chunk(c, carry):
-            lanes = pl.ds(pl.multiple_of(c * 256, 256), 256)
+        def chunk(c):
+            lanes = slice(c * PART, (c + 1) * PART)
             dy = g("cot")[:, lanes]
             if m is SEA:
                 dy = dy * r.wetf[:, lanes]
@@ -583,9 +584,9 @@
             dmean = jnp.mean(dn, axis=0, keepdims=True)
             dproj = jnp.mean(dn * x, axis=0, keepdims=True)
             g("dmr")[1, :, lanes] = g("rstd")[step, :, lanes] * (dn - dmean - x * dproj)
-            return carry
-
-        lax.fori_loop(0, SL // 256, chunk, 0)
+
+        for c in range(SL // PART):
+            chunk(c)
         fp, dmr = g("fp"), g("dmr")
         dw = g("dw")[...]
         for row in range(rows):

time: 85.4 us -> 74.7 us (0.87)
  Pallas kernels: 84.5 us -> 73.8 us
    pallas_call x1, Pallas kernels: 82.2 us -> 71.5 us  [body(): pl.pallas_call(lambda *refs: kernel(n, *refs), out_shape=fields + [jax.Sh...]
where the time goes in v3:
time: 74.7 us; the launch traced here: 74.6 us
  Pallas kernels  73.8 us (99%)
  between operations  0.82 us (1%)
    pallas_call x1, Pallas kernels, body(): pl.pallas_call(lambda *refs: kernel(n, *refs), out_shape=fields + [jax.Sh...  71.5 us
    pallas_call x1, Pallas kernels, body(): pl.pallas_call(lambda *refs: finish(n, *refs), out_shape=fields + [jax.Sh...  2.3 us

profile of v3, /device:TPU:1, one launch (start us, length us, event | category | flops | bytes accessed | tf_op | source)
XLA Modules:
  0.0 74.6 jit_solution(15026897168648430077)
XLA Ops:
  0.7 71.5 %coupled.1 = (f32[8,8,128]{2,1,0:T(8,128)}, f32[48,2,512]{2,1,0:T(2,128)}, f32[8,8,128]{2,1,0:T(8,128)}, f32[48,2,512]{2,1,0:T(2,128)}, f32[4,8,128]{2,1,0:T(8,128)}, /*index=5*/bf16[2,4,8,16,128]{4,3,2,1,0:T(8,128)(2,1)}) custom-call(f32[8,8,128]{2,1,0:T(8,128)} %refs_0_.1, f32[48,2,512]{2,1,0:T(2,128)} %refs_1_.1, f32[4,8,128]{2,1,0:T(8,128)} %refs_2_.1, ...), custom_call_target="tpu_custom_call" | custom-call | tf_op jit(solution)/shard_map/coupled/pallas_call | solution.py:959
  72.1 2.3 %finish.1 = (f32[8,8,128]{2,1,0:T(8,128)}, f32[48,2,512]{2,1,0:T(2,128)}, f32[8,8,128]{2,1,0:T(8,128)}, f32[48,2,512]{2,1,0:T(2,128)}, f32[4,8,128]{2,1,0:T(8,12...) custom-call(f32[8,8,128]{2,1,0:T(8,128)} %get-tuple-element.36.refs_, ...), custom_call_target="tpu_custom_call" | custom-call | tf_op jit(solution)/shard_map/finish/pallas_call | solution.py:972
